TPU v7x, 32 devices: a whole 2x2x4 slice. The times are simulated.
32 devices in a mesh: batch: 8 (over y, x, core), mp: 4 (over z).
Axes of the slice: x: 2, y: 2, z: 4, core: 2. Of those that a mesh axis runs over, the one named last changes fastest.
Arguments:
- tokens: bfloat16 [16384, 768], P(('batch', 'mp')), may hold values from -6 to 6
- cotangent: bfloat16 [16384, 768], P(('batch', 'mp')), may hold values from -6 to 6
- lengths: int32 [8, 6], P('batch'), may hold values from 1 to 1024, 2048 in all within a row
- buckets: int32 [2047], replicated, may hold values from 0 to 31
- w_query: bfloat16 [768, 768], P(None, 'mp'), may hold values from -0.046875 to 0.046875
- w_key: bfloat16 [768, 768], P(None, 'mp'), may hold values from -0.21875 to 0.21875
- w_value: bfloat16 [768, 768], P(None, 'mp'), may hold values from -0.21875 to 0.21875
- w_out: bfloat16 [768, 768], P('mp'), may hold values from -0.625 to 0.625
- w_gate: bfloat16 [768, 2048], P(None, 'mp'), may hold values from -0.21875 to 0.21875
- w_up: bfloat16 [768, 2048], P(None, 'mp'), may hold values from -0.21875 to 0.21875
- w_down: bfloat16 [2048, 768], P('mp'), may hold values from -0.125 to 0.125
- rel_table: float32 [32, 12], P(None, 'mp'), may hold values from -3 to 3
- gain_one: float32 [768], replicated, may hold values from 0.25 to 1.75
- gain_two: float32 [768], replicated, may hold values from 0.25 to 1.75
Outputs:
- layer_out: bfloat16 [16384, 768], P(('batch', 'mp'))
- grad_tokens: bfloat16 [16384, 768], P(('batch', 'mp'))
- grad_w_query: float32 [768, 768], P(None, 'mp')
- grad_w_key: float32 [768, 768], P(None, 'mp')
- grad_w_value: float32 [768, 768], P(None, 'mp')
- grad_w_out: float32 [768, 768], P('mp')
- grad_w_gate: float32 [768, 2048], P(None, 'mp')
- grad_w_up: float32 [768, 2048], P(None, 'mp')
- grad_w_down: float32 [2048, 768], P('mp')
- grad_rel_table: float32 [32, 12], P(None, 'mp')
- grad_gain_one: float32 [768], replicated
- grad_gain_two: float32 [768], replicated
- stat_model: float32 [5, 768], replicated
- stat_heads: float32 [4, 768], P(None, 'mp')
- stat_hidden: float32 [3, 2048], P(None, 'mp')
- stat_ffn_rows: float32 [2, 768], replicated
Inputs may be any that keep to these rules, and one draw needn't show every extreme that they name: Each row's entries sum to 2048; the first 5 are the lengths of its sequences in order, the last is the padding at its end; some entry of each row is exactly 1024. `buckets`: entry o holds the bucket of the relative offset o - 1023.
All inputs are finite; a program needn't handle non-finite values.
Results may differ from a plain program's by a relative error of at most 0.02.
Values may be sent and summed in bfloat16 or wider, within the bound.
A program may use at most 384 MiB of HBM per device.

v0:
```python
import jax
import jax.numpy as jnp
from jax import lax
from jax.sharding import PartitionSpec as P

QB = 512


EPS = 1e-06
NEG = -1000000000.0
TINY = 1e-30
HIGH = lax.Precision.HIGHEST


def norm_rows(values, gain_vec):
    return values * lax.rsqrt(jnp.mean(values * values, axis=-1, keepdims=True) + EPS) * gain_vec


def contract_rows(left_side, right_side):
    return lax.dot_general(
        left_side, right_side, (((0,), (0,)), ((), ())), preferred_element_type=jnp.float32
    )


def contract_cols(left_side, right_side):
    return lax.dot_general(
        left_side, right_side, (((1,), (1,)), ((), ())), preferred_element_type=jnp.float32
    )


def segment_rows(lengths, row_width):
    ends_at = jnp.cumsum(lengths, axis=1)
    places = jnp.arange(row_width, dtype=jnp.int32)
    return jnp.sum((places[None, :, None] >= ends_at[:, None, :]).astype(jnp.int32), axis=2)


def spread_diagonals(bias_table, height, row_width):
    head_count = bias_table.shape[0]
    span = height + row_width
    padded = jnp.pad(bias_table, ((0, 0), (0, 1)))
    tiled_rows = jnp.broadcast_to(padded[:, None, :], (head_count, height, span)).reshape(
        head_count, height * span
    )
    sheared = lax.slice_in_dim(tiled_rows, height - 1, height - 1 + height * (span - 1), axis=1)
    return sheared.reshape(head_count, height, span - 1)[:, :, :row_width]


def sum_diagonals(block_values, height, row_width):
    head_count = block_values.shape[0]
    span = height + row_width
    padded = jnp.pad(block_values, ((0, 0), (0, 0), (height, 0))).reshape(head_count, height * span)
    padded = jnp.pad(padded, ((0, 0), (0, height)))
    sheared = padded.reshape(head_count, height, span + 1)[:, :, 1:span]
    return jnp.sum(sheared, axis=1)


def bucket_onehot(buckets, start_row, height, row_width, bucket_count):
    limit = (buckets.shape[0] + 1) // 2
    offsets = (
        jnp.arange(height + row_width - 1, dtype=jnp.int32) - (height - 1) - start_row + limit - 1
    )
    kind_ids = buckets[jnp.clip(offsets, 0, 2 * limit - 2)]
    return (kind_ids[:, None] == jnp.arange(bucket_count, dtype=jnp.int32)[None, :]).astype(
        jnp.float32
    )


def block_bias(rel_table, buckets, start_row, height, row_width):
    onehot = bucket_onehot(buckets, start_row, height, row_width, rel_table.shape[0])
    bias_table = jnp.dot(onehot, rel_table, precision=HIGH).T
    return spread_diagonals(bias_table, height, row_width)


def block_scores(queries, key_rows, segments, token_valid, bias_block, start_row):
    height = queries.shape[1]
    row_width = key_rows.shape[1]
    scores = jnp.einsum("hqd,hkd->hqk", queries, key_rows, preferred_element_type=jnp.float32)
    scores = scores + bias_block
    row_index = start_row + jnp.arange(height, dtype=jnp.int32)
    col_index = jnp.arange(row_width, dtype=jnp.int32)
    seg_rows = lax.dynamic_slice_in_dim(segments, start_row, height)
    allowed = (seg_rows[:, None] == segments[None, :]) & token_valid[None, :] | (
        row_index[:, None] == col_index[None, :]
    )
    return jnp.where(allowed[None], scores, NEG)


def attend_row(row_qkv, segments, token_valid, bias_all):
    row_q = row_qkv[0]
    row_k = row_qkv[1]
    row_v = row_qkv[2]
    row_width = row_k.shape[1]
    block_ids = jnp.arange(row_width // QB, dtype=jnp.int32)

    def one_block(block_id):
        start_row = block_id * QB
        queries = lax.dynamic_slice_in_dim(row_q, start_row, QB, 1)
        bias_block = lax.dynamic_index_in_dim(bias_all, block_id, 0, keepdims=False)
        scores = block_scores(queries, row_k, segments, token_valid, bias_block, start_row)
        row_max = jnp.max(scores, axis=-1, keepdims=True)
        weights = jnp.exp(scores - row_max)
        totals = jnp.sum(weights, axis=-1, keepdims=True)
        probs_low = (weights / totals).astype(jnp.bfloat16)
        context = jnp.einsum(
            "hqk,hkd->hqd", probs_low, row_v, preferred_element_type=jnp.float32
        ).astype(jnp.bfloat16)
        return (context, (row_max + jnp.log(totals))[:, :, 0])

    return lax.map(one_block, block_ids)


def attend_back(
    row_qkv, grad_blocks, segments, token_valid, log_sums, bias_all, rel_table, buckets
):
    row_q = row_qkv[0]
    row_k = row_qkv[1]
    row_v = row_qkv[2]
    head_count, row_width, head_dim = row_k.shape
    block_ids = jnp.arange(row_width // QB, dtype=jnp.int32)

    def one_block(carry, entry):
        grad_key, grad_value, grad_rel = carry
        block_id, block_lse, grad_ctx = entry
        start_row = block_id * QB
        queries = lax.dynamic_slice_in_dim(row_q, start_row, QB, 1)
        bias_block = lax.dynamic_index_in_dim(bias_all, block_id, 0, keepdims=False)
        scores = block_scores(queries, row_k, segments, token_valid, bias_block, start_row)
        probs = jnp.exp(scores - block_lse[:, :, None])
        probs_low = probs.astype(jnp.bfloat16)
        grad_value = grad_value + jnp.einsum(
            "hqk,hqd->hkd", probs_low, grad_ctx, preferred_element_type=jnp.float32
        )
        grad_probs = jnp.einsum("hqd,hkd->hqk", grad_ctx, row_v, preferred_element_type=jnp.float32)
        grad_scores = (
            probs * (grad_probs - jnp.sum(probs * grad_probs, axis=-1, keepdims=True))
        ).astype(jnp.bfloat16)
        grad_query = jnp.einsum(
            "hqk,hkd->hqd", grad_scores, row_k, preferred_element_type=jnp.float32
        )
        grad_key = grad_key + jnp.einsum(
            "hqk,hqd->hkd", grad_scores, queries, preferred_element_type=jnp.float32
        )
        diagonals = sum_diagonals(grad_scores.astype(jnp.float32), QB, row_width)
        onehot = bucket_onehot(buckets, start_row, QB, row_width, rel_table.shape[0])
        grad_rel = grad_rel + jnp.dot(onehot.T, diagonals.T, precision=HIGH)
        return ((grad_key, grad_value, grad_rel), grad_query.astype(jnp.bfloat16))

    zero_rows = jnp.zeros((head_count, row_width, head_dim), jnp.float32)
    initial = (zero_rows, zero_rows, jnp.zeros(rel_table.shape, jnp.float32))
    (grad_key, grad_value, grad_rel), grad_query = lax.scan(
        one_block, initial, (block_ids, log_sums, grad_blocks)
    )
    return (grad_query, grad_key.astype(jnp.bfloat16), grad_value.astype(jnp.bfloat16), grad_rel)


def on_device(
    tokens,
    cotangent,
    lengths,
    buckets,
    w_query,
    w_key,
    w_value,
    w_out,
    w_gate,
    w_up,
    w_down,
    rel_table,
    gain_one,
    gain_two,
):
    rows_dev = lengths.shape[0]
    own_rows = tokens.shape[0]
    model_width = tokens.shape[1]
    all_rows = own_rows * lax.axis_size("mp")
    row_width = all_rows // rows_dev
    block_count = row_width // QB
    head_count = rel_table.shape[1]
    inner_width = w_query.shape[1]
    head_dim = inner_width // head_count
    hidden_width = w_gate.shape[1]
    segments = segment_rows(lengths, row_width)
    token_valid = segments < lengths.shape[1] - 1
    w_joined = jnp.concatenate([w_query, w_key, w_value], axis=1)
    w_heads = w_joined.reshape(model_width, 3, head_count, head_dim)

    def bias_of(block_id):
        return block_bias(rel_table, buckets, block_id * QB, QB, row_width)

    bias_all = lax.map(bias_of, jnp.arange(block_count, dtype=jnp.int32))
    inputs = tokens.astype(jnp.float32)
    normed_one = norm_rows(inputs, gain_one).astype(jnp.bfloat16)
    rows_one = lax.all_gather(normed_one, "mp", axis=0, tiled=True)
    projected = jnp.einsum(
        "rtd,dshe->rshte",
        rows_one.reshape(rows_dev, row_width, model_width),
        w_heads,
        preferred_element_type=jnp.float32,
    ).astype(jnp.bfloat16)

    def forward_row(entry):
        return attend_row(entry[0], entry[1], entry[2], bias_all)

    context_heads, log_sums = lax.map(forward_row, (projected, segments, token_valid))
    context = jnp.transpose(context_heads, (0, 1, 3, 2, 4)).reshape(all_rows, inner_width)
    attn_out = lax.psum_scatter(
        jnp.dot(context, w_out, preferred_element_type=jnp.float32).astype(jnp.bfloat16),
        "mp",
        scatter_dimension=0,
        tiled=True,
    ).astype(jnp.float32)
    middle = inputs + attn_out
    normed_two = norm_rows(middle, gain_two).astype(jnp.bfloat16)
    rows_two = lax.all_gather(normed_two, "mp", axis=0, tiled=True)
    gate_pre = jnp.dot(rows_two, w_gate, preferred_element_type=jnp.float32)
    up_proj = jnp.dot(rows_two, w_up, preferred_element_type=jnp.float32)
    hidden = (jax.nn.gelu(gate_pre, approximate=True) * up_proj).astype(jnp.bfloat16)
    ffn_out = lax.psum_scatter(
        jnp.dot(hidden, w_down, preferred_element_type=jnp.float32).astype(jnp.bfloat16),
        "mp",
        scatter_dimension=0,
        tiled=True,
    ).astype(jnp.float32)
    layer_out = (middle + ffn_out).astype(jnp.bfloat16)
    rows_cot = lax.all_gather(cotangent, "mp", axis=0, tiled=True)
    grad_hidden = contract_cols(rows_cot, w_down)
    grad_w_down = contract_rows(hidden, rows_cot)

    def gated_unit(gate_in, up_in):
        return jax.nn.gelu(gate_in, approximate=True) * up_in

    grad_gate, grad_up = jax.vjp(gated_unit, gate_pre, up_proj)[1](grad_hidden)
    grad_gate = grad_gate.astype(jnp.bfloat16)
    grad_up = grad_up.astype(jnp.bfloat16)
    grad_w_gate = contract_rows(rows_two, grad_gate)
    grad_w_up = contract_rows(rows_two, grad_up)
    gate_part = contract_cols(grad_gate, w_gate)
    grad_norm_two = lax.psum_scatter(
        (gate_part + contract_cols(grad_up, w_up)).astype(jnp.bfloat16),
        "mp",
        scatter_dimension=0,
        tiled=True,
    ).astype(jnp.float32)
    grad_middle_part, gain_two_part = jax.vjp(norm_rows, middle, gain_two)[1](grad_norm_two)
    grad_middle = cotangent.astype(jnp.float32) + grad_middle_part
    grad_attn = grad_middle.astype(jnp.bfloat16)
    rows_grad = lax.all_gather(grad_attn, "mp", axis=0, tiled=True)
    grad_context = contract_cols(rows_grad, w_out).astype(jnp.bfloat16)
    grad_w_out = contract_rows(context, rows_grad)
    grad_blocks = jnp.transpose(
        grad_context.reshape(rows_dev, block_count, QB, head_count, head_dim), (0, 1, 3, 2, 4)
    )

    def backward_row(entry):
        return attend_back(
            entry[0], entry[1], entry[2], entry[3], entry[4], bias_all, rel_table, buckets
        )

    grad_query, grad_key, grad_value, grad_rel = lax.map(
        backward_row, (projected, grad_blocks, segments, token_valid, log_sums)
    )
    grad_query = jnp.transpose(grad_query, (0, 1, 3, 2, 4)).reshape(all_rows, inner_width)
    grad_key = jnp.transpose(grad_key, (0, 2, 1, 3)).reshape(all_rows, inner_width)
    grad_value = jnp.transpose(grad_value, (0, 2, 1, 3)).reshape(all_rows, inner_width)
    grad_joined = jnp.concatenate([grad_query, grad_key, grad_value], axis=1)
    grad_rel = jnp.sum(grad_rel, axis=0)
    grad_w_joined = contract_rows(rows_one, grad_joined)
    grad_norm_one = lax.psum_scatter(
        contract_cols(grad_joined, w_joined).astype(jnp.bfloat16),
        "mp",
        scatter_dimension=0,
        tiled=True,
    ).astype(jnp.float32)
    grad_input_part, gain_one_part = jax.vjp(norm_rows, inputs, gain_one)[1](grad_norm_one)
    grad_tokens = (grad_middle + grad_input_part).astype(jnp.bfloat16)
    grad_w_query = grad_w_joined[:, :inner_width]
    grad_w_key = grad_w_joined[:, inner_width : 2 * inner_width]
    grad_w_value = grad_w_joined[:, 2 * inner_width :]
    summed = lax.psum(
        (
            grad_w_query,
            grad_w_key,
            grad_w_value,
            grad_w_out,
            grad_w_gate,
            grad_w_up,
            grad_w_down,
            grad_rel,
            gain_one_part,
            gain_two_part,
        ),
        "batch",
    )
    scale = lax.rsqrt(jnp.float32(rows_dev * row_width * lax.axis_size("batch")))
    scaled = tuple((member * scale for member in summed))
    squares = tuple((member * member for member in scaled[:7]))
    model_side = jnp.stack(
        [
            jnp.sum(squares[0], axis=1),
            jnp.sum(squares[1], axis=1),
            jnp.sum(squares[2], axis=1),
            jnp.sum(squares[4], axis=1),
            jnp.sum(squares[5], axis=1),
            jnp.sum(squares[3], axis=0),
            jnp.sum(squares[6], axis=0),
        ]
    )
    model_side, gain_grads = lax.psum((model_side, jnp.stack([scaled[8], scaled[9]])), "mp")
    inner_total = float(inner_width * lax.axis_size("mp"))
    hidden_total = float(hidden_width * lax.axis_size("mp"))
    counts = jnp.array(
        [
            inner_total,
            inner_total,
            inner_total,
            hidden_total,
            hidden_total,
            inner_total,
            hidden_total,
        ],
        jnp.float32,
    )
    stat_every = model_side / counts[:, None] + TINY
    stat_model = jnp.concatenate([stat_every[:3], stat_every[5:]], axis=0)
    stat_ffn_rows = stat_every[3:5]
    stat_heads = jnp.stack(
        [
            jnp.mean(squares[0] + TINY, axis=0),
            jnp.mean(squares[1] + TINY, axis=0),
            jnp.mean(squares[2] + TINY, axis=0),
            jnp.mean(squares[3] + TINY, axis=1),
        ]
    )
    stat_hidden = jnp.stack(
        [
            jnp.mean(squares[4] + TINY, axis=0),
            jnp.mean(squares[5] + TINY, axis=0),
            jnp.mean(squares[6] + TINY, axis=1),
        ]
    )
    return (
        layer_out,
        grad_tokens,
        scaled[0],
        scaled[1],
        scaled[2],
        scaled[3],
        scaled[4],
        scaled[5],
        scaled[6],
        scaled[7],
        gain_grads[0],
        gain_grads[1],
        stat_model,
        stat_heads,
        stat_hidden,
        stat_ffn_rows,
    )


def solution(mesh):
    in_specs = (
        P(("batch", "mp"), None),
        P(("batch", "mp"), None),
        P("batch", None),
        P(),
        P(None, "mp"),
        P(None, "mp"),
        P(None, "mp"),
        P("mp", None),
        P(None, "mp"),
        P(None, "mp"),
        P("mp", None),
        P(None, "mp"),
        P(),
        P(),
    )
    out_specs = (
        P(("batch", "mp"), None),
        P(("batch", "mp"), None),
        P(None, "mp"),
        P(None, "mp"),
        P(None, "mp"),
        P("mp", None),
        P(None, "mp"),
        P(None, "mp"),
        P("mp", None),
        P(None, "mp"),
        P(),
        P(),
        P(),
        P(None, "mp"),
        P(None, "mp"),
        P(),
    )
    return jax.shard_map(
        on_device, mesh=mesh, in_specs=in_specs, out_specs=out_specs, check_vma=False
    )
```

profile of v0, /device:TPU:0, one launch (start us, length us, event | category | flops | bytes accessed | tf_op | source)
XLA Modules:
  0.0 1821.5 jit_solution(3036207269416536661)
XLA Ops:
  12.3 583.3 %while.69 = (s32[]{:T(128)}, f32[4,3,512,2048]{3,2,1,0:T(8,128)}, s32[4]{0:T(128)S(1)}, s32[2047]{0:T(1024)S(1)}, f32[32,3]{0,1:T(4,128)S(1)}, /*index=5*/s32[]{:T(128)}, s32[1]{0:T(128)}, f32[]{:T(128)}) while((s32[]{:T(128)}, f32[4,3,512,2048]{3,2,1,0:T(8,128)}, s32[4]{0:T(128)S(1)}, s32[2047]{0:T(1024)S(1)}, f32[32,3]{0,1:T(4,128)S(1)}, ...), condition=%wide.region_2.3_spmd, body=%wide.region_1.2_spmd.sunk | while | flops 3050844 | bytes 166884304 | solution.py:190
  13.6 13.6 gather_fusion
  31.0 33.0 %copy.47 = f32[1,3,512,2560]{3,1,2,0:T(4,128)S(1)} copy(f32[1,3,512,2560]{3,2,1,0:T(8,128)S(1)} %broadcast_bitcast_fusion.2) | data formatting | bytes 31457280 | tf_op jit(solution)/shard_map/while
  64.0 13.6 slice.129
  77.5 44.4 %reshape.523 = f32[3930624]{0:T(1024)} reshape(f32[3,1310208]{1,0:T(4,128)} %slice.129) | data formatting | bytes 31444992 | tf_op jit(solution)/shard_map/while
  121.9 23.1 %reshape.524 = f32[3,512,2559]{2,1,0:T(8,128)} reshape(f32[3930624]{0:T(1024)} %reshape.523) | data formatting | bytes 31444992 | tf_op jit(solution)/shard_map/while/body/eval_jaxpr/reshape | solution.py:45
  145.0 11.3 fusion.146
  157.7 13.6 gather_fusion
  175.0 33.0 %copy.47 = f32[1,3,512,2560]{3,1,2,0:T(4,128)S(1)} copy(f32[1,3,512,2560]{3,2,1,0:T(8,128)S(1)} %broadcast_bitcast_fusion.2) | data formatting | bytes 31457280 | tf_op jit(solution)/shard_map/while
  208.0 13.6 slice.129
  221.6 44.4 %reshape.523 = f32[3930624]{0:T(1024)} reshape(f32[3,1310208]{1,0:T(4,128)} %slice.129) | data formatting | bytes 31444992 | tf_op jit(solution)/shard_map/while
  266.0 23.1 %reshape.524 = f32[3,512,2559]{2,1,0:T(8,128)} reshape(f32[3930624]{0:T(1024)} %reshape.523) | data formatting | bytes 31444992 | tf_op jit(solution)/shard_map/while/body/eval_jaxpr/reshape | solution.py:45
  289.1 11.2 fusion.146
  301.6 13.6 gather_fusion
  319.0 33.0 %copy.47 = f32[1,3,512,2560]{3,1,2,0:T(4,128)S(1)} copy(f32[1,3,512,2560]{3,2,1,0:T(8,128)S(1)} %broadcast_bitcast_fusion.2) | data formatting | bytes 31457280 | tf_op jit(solution)/shard_map/while
  352.0 13.6 slice.129
  365.5 44.4 %reshape.523 = f32[3930624]{0:T(1024)} reshape(f32[3,1310208]{1,0:T(4,128)} %slice.129) | data formatting | bytes 31444992 | tf_op jit(solution)/shard_map/while
  410.0 23.1 %reshape.524 = f32[3,512,2559]{2,1,0:T(8,128)} reshape(f32[3930624]{0:T(1024)} %reshape.523) | data formatting | bytes 31444992 | tf_op jit(solution)/shard_map/while/body/eval_jaxpr/reshape | solution.py:45
  433.1 11.3 fusion.146
  445.7 13.6 gather_fusion
  463.1 33.0 %copy.47 = f32[1,3,512,2560]{3,1,2,0:T(4,128)S(1)} copy(f32[1,3,512,2560]{3,2,1,0:T(8,128)S(1)} %broadcast_bitcast_fusion.2) | data formatting | bytes 31457280 | tf_op jit(solution)/shard_map/while
  496.1 13.6 slice.129
  509.6 44.4 %reshape.523 = f32[3930624]{0:T(1024)} reshape(f32[3,1310208]{1,0:T(4,128)} %slice.129) | data formatting | bytes 31444992 | tf_op jit(solution)/shard_map/while
  554.0 23.1 %reshape.524 = f32[3,512,2559]{2,1,0:T(8,128)} reshape(f32[3930624]{0:T(1024)} %reshape.523) | data formatting | bytes 31444992 | tf_op jit(solution)/shard_map/while/body/eval_jaxpr/reshape | solution.py:45
  577.1 11.2 fusion.146
  602.9 65.9 %while.70 = (s32[]{:T(128)}, bf16[4,3,512,64]{2,3,1,0:T(8,128)(2,1)}, f32[4,3,512]{2,1,0:T(4,128)S(1)}, s32[4]{0:T(128)S(1)}, s32[2048]{0:T(1024)S(1)}, /*index=...) while((s32[]{:T(128)}, ...), condition=%wide.region_8.9_spmd, body=%wide.region_5.8_spmd.sunk | while | flops 834763776 | bytes 54471420 | solution.py:109
  674.4 63.1 %reduce-scatter.5.cloned.1.call-done = bf16[512,768]{1,0:T(8,128)(2,1)} async-done(((bf16[2048,768]{1,0:T(8,128)(2,1)}), bf16[512,768]{1,0:T(8,128)(2,1)}) %reduce-scatter.5.cloned.1.call-update) | async-done | bytes 786448 | tf_op jit(solution)/shard_map/reduce_scatter | solution.py:206
  742.1 62.8 %all-gather.7.cloned.1.call-done = bf16[2048,768]{1,0:T(8,128)(2,1)} async-done(((bf16[512,768]{1,0:T(8,128)(2,1)}), bf16[2048,768]{1,0:T(8,128)(2,1)}) %all-gather.7.cloned.1.call-update) | async-done | bytes 3145744 | tf_op jit(solution)/shard_map/all_gather | solution.py:214
  814.9 53.7 %all-gather.9.cloned.1.call-done = bf16[2048,768]{1,0:T(8,128)(2,1)} async-done(((bf16[512,768]{1,0:T(8,128)(2,1)}), bf16[2048,768]{1,0:T(8,128)(2,1)}) %all-gather.9.cloned.1.call-update) | async-done | bytes 3145744 | tf_op jit(solution)/shard_map/all_gather | solution.py:225
  868.6 8.8 multiply_convert_fusion.1
  882.9 59.0 %reduce-scatter.9.cloned.1.call-done = bf16[512,768]{1,0:T(8,128)(2,1)} async-done(((bf16[2048,768]{1,0:T(8,128)(2,1)}), bf16[512,768]{1,0:T(8,128)(2,1)}) %reduce-scatter.9.cloned.1.call-update) | async-done | bytes 786448 | tf_op jit(solution)/shard_map/reduce_scatter | solution.py:238
  960.2 51.2 %all-gather.11.cloned.1.call-done = bf16[2048,768]{1,0:T(8,128)(2,1)} async-done(((bf16[512,768]{1,0:T(8,128)(2,1)}), bf16[2048,768]{1,0:T(8,128)(2,1)}) %all-gather.11.cloned.1.call-update) | async-done | bytes 3145744 | tf_op jit(solution)/shard_map/all_gather | solution.py:247
  1019.7 542.2 %while.71 = (s32[]{:T(128)}, f32[3,2048,64]{1,2,0:T(8,128)}, f32[3,2048,64]{1,2,0:T(8,128)}, f32[32,3]{0,1:T(4,128)S(1)}, bf16[4,3,512,64]{2,3,1,0:T(8,128)(2,1)...) while((s32[]{:T(128)}, f32[3,2048,64]{1,2,0:T(8,128)}, ...), condition=%wide.region_17.18_spmd.clone, body=%wide.region_14.17_spmd.clone.sunk | while | flops 2058346496 | bytes 228987440 | solution.py:150
  1032.0 13.8 multiply_reduce_fusion.10
  1045.8 8.9 multiply_convert_fusion.5
  1059.8 11.6 copy.48
  1077.4 14.1 reshape.527
  1091.5 22.0 %reshape.528 = bf16[3,512,2561]{2,1,0:T(8,128)(2,1)} reshape(bf16[3933696]{0:T(1024)(128)(2,1)} %reshape.527) | data formatting | bytes 15734784 | tf_op jit(solution)/shard_map/while/body/eval_jaxpr/while/body/eval_jaxpr/reshape | solution.py:53
  1120.6 13.6 gather_fusion.1
  1164.7 13.8 multiply_reduce_fusion.10
  1178.6 8.9 multiply_convert_fusion.5
  1192.6 11.6 copy.48
  1210.2 14.1 reshape.527
  1224.3 21.9 %reshape.528 = bf16[3,512,2561]{2,1,0:T(8,128)(2,1)} reshape(bf16[3933696]{0:T(1024)(128)(2,1)} %reshape.527) | data formatting | bytes 15734784 | tf_op jit(solution)/shard_map/while/body/eval_jaxpr/while/body/eval_jaxpr/reshape | solution.py:53
  1253.4 13.6 gather_fusion.1
  1278.9 7.5 fusion.165
  1298.4 13.8 multiply_reduce_fusion.10
  1312.2 8.9 multiply_convert_fusion.5
  1326.2 11.6 copy.48
  1344.0 14.1 reshape.527
  1358.1 21.7 %reshape.528 = bf16[3,512,2561]{2,1,0:T(8,128)(2,1)} reshape(bf16[3933696]{0:T(1024)(128)(2,1)} %reshape.527) | data formatting | bytes 15734784 | tf_op jit(solution)/shard_map/while/body/eval_jaxpr/while/body/eval_jaxpr/reshape | solution.py:53
  1387.0 13.6 gather_fusion.1
  1412.6 7.5 fusion.165
  1432.2 13.8 multiply_reduce_fusion.10
  1446.0 8.9 multiply_convert_fusion.5
  1460.1 11.6 copy.48
  1477.6 14.1 reshape.527
  1491.7 22.0 %reshape.528 = bf16[3,512,2561]{2,1,0:T(8,128)(2,1)} reshape(bf16[3933696]{0:T(1024)(128)(2,1)} %reshape.527) | data formatting | bytes 15734784 | tf_op jit(solution)/shard_map/while/body/eval_jaxpr/while/body/eval_jaxpr/reshape | solution.py:53
  1520.9 13.6 gather_fusion.1
  1581.9 102.5 %all-reduce.8.cloned.1.call-done = (f32[768,192]{0,1:T(8,128)}, f32[768,192]{0,1:T(8,128)}, f32[768,192]{0,1:T(8,128)}, f32[192,768]{1,0:T(8,128)}, f32[768,512]...) async-done(((f32[768,192]{0,1:T(8,128)}, f32[768,192]{0,1:T(8,128)}, f32[768,192]{0,1:T(8,128)}, f32[192,768]{1,0:T(8,128)}, f32[768,512]{1,0:T(8,128)}, ...) | async-done | bytes 7077904 | tf_op jit(solution)/shard_map/psum | solution.py:279
  1694.3 52.8 %reduce-scatter.11.cloned.1.call-done = bf16[512,768]{1,0:T(8,128)(2,1)} async-done(((bf16[2048,768]{1,0:T(8,128)(2,1)}), bf16[512,768]{1,0:T(8,128)(2,1)}) %reduce-scatter.11.cloned.1.call-update) | async-done | bytes 786448 | tf_op jit(solution)/shard_map/reduce_scatter | solution.py:268
  1749.0 24.7 %all-reduce.3 = (f32[32,3]{0,1:T(4,128)S(1)}, f32[768]{0:T(1024)S(1)}, f32[768]{0:T(1024)S(1)}) all-reduce(f32[32,3]{0,1:T(4,128)S(1)} %get-tuple-element.535, f32[768]{0:T(1024)S(1)} %copy-done.42, f32[768]{0:T(1024)S(1)} %get-tuple-element.592), channel_id=1, replica_groups=mesh['batch'=8,'mp'=4] {'batch'}, use_global_device_ids=true, to_apply=%region_27.28 | all-reduce | flops 1632 | bytes 13056 | tf_op jit(solution)/shard_map/psum | solution.py:279
  1773.7 20.0 %all-reduce.5 = (f32[2,768]{1,0:T(2,128)S(1)}, f32[7,768]{1,0:T(8,128)S(1)}) all-reduce(f32[2,768]{1,0:T(2,128)S(1)} %pad_maximum_fusion.5, f32[7,768]{1,0:T(8,128)S(1)} %stack.56), channel_id=1, replica_groups=mesh['batch'=8,'mp'=4] {'mp'}, use_global_device_ids=true, to_apply=%region_32.33 | all-reduce | flops 6912 | bytes 55296 | tf_op jit(solution)/shard_map/psum | solution.py:308
  1796.2 14.4 reduce-scatter.7.cloned.1.call-done
  (323 shorter events, 346.6 us)
Async XLA Ops:
  7.2 861.4 %copy-start = (bf16[512,768]{1,0:T(8,128)(2,1)S(1)}, bf16[512,768]{1,0:T(8,128)(2,1)}, u32[]{:S(2)}) copy-start(bf16[512,768]{1,0:T(8,128)(2,1)} %param.31) | copy-start | bytes 2359300
  7.2 5.0 copy-start.1
  7.2 5.0 copy-start.46
  7.2 588.8 %all-gather.5.cloned.1.call-start = ((), (), s32[]{:S(2)}) async-start(), calls=%async_computation.4 | async-start | bytes 3932160 | tf_op jit(solution)/shard_map/all_gather | solution.py:193
  8.7 0.6 copy-start.40
  9.3 0.6 copy-start.36
  12.2 725.3 %reduce-scatter.5.cloned.1.call-start = ((), (), s32[]{:S(2)}) async-start(), calls=%async_computation.5 | async-start | bytes 3932160 | tf_op jit(solution)/shard_map/reduce_scatter | solution.py:206
  12.2 583.3 %copy-start.47 = (s32[1,6]{1,0:T(1,128)S(1)}, s32[1,6]{1,0:T(1,128)}, u32[]{:S(2)}) copy-start(s32[1,6]{1,0:T(1,128)} %param.23) | copy-start | bytes 76
  12.3 583.7 %copy-start.25 = (bf16[768,192]{0,1:T(8,128)(2,1)S(1)}, bf16[768,192]{0,1:T(8,128)(2,1)}, u32[]{:S(2)}) copy-start(bf16[768,192]{0,1:T(8,128)(2,1)} %param.25) | copy-start | bytes 884740
  12.3 583.7 %copy-start.26 = (bf16[768,192]{0,1:T(8,128)(2,1)S(1)}, bf16[768,192]{0,1:T(8,128)(2,1)}, u32[]{:S(2)}) copy-start(bf16[768,192]{0,1:T(8,128)(2,1)} %param.26) | copy-start | bytes 884740
  12.3 583.7 %copy-start.27 = (bf16[768,192]{0,1:T(8,128)(2,1)S(1)}, bf16[768,192]{0,1:T(8,128)(2,1)}, u32[]{:S(2)}) copy-start(bf16[768,192]{0,1:T(8,128)(2,1)} %param.27) | copy-start | bytes 884740
  596.0 0.9 copy-start.30
  668.8 2.9 copy-start.28
  670.8 0.9 copy-start.12
  674.3 63.2 %copy-start.5 = (bf16[512,768]{1,0:T(8,128)(2,1)S(1)}, bf16[512,768]{1,0:T(8,128)(2,1)}, u32[]{:S(2)}) copy-start(bf16[512,768]{1,0:T(8,128)(2,1)} %param.21) | copy-start | bytes 2359300
  674.3 64.6 %copy-start.31 = (f32[768]{0:T(1024)S(1)}, f32[768]{0:T(1024)}, u32[]{:S(2)}) copy-start(f32[768]{0:T(1024)} %param.34) | copy-start | bytes 9220
  674.3 130.6 %all-gather.7.cloned.1.call-start = ((), (), s32[]{:S(2)}) async-start(), calls=%async_computation.6 | async-start | bytes 3932160 | tf_op jit(solution)/shard_map/all_gather | solution.py:214
  738.9 205.7 %copy-start.33 = (f32[512]{0:T(512)}, f32[512]{0:T(512)S(1)}, u32[]{:S(2)}) copy-start(f32[512]{0:T(512)S(1)} %fusion.69) | copy-start | bytes 6148
  741.3 127.3 %all-gather.9.cloned.1.call-start = ((), (), s32[]{:S(2)}) async-start(), calls=%async_computation.8 | async-start | bytes 3932160 | tf_op jit(solution)/shard_map/all_gather | solution.py:225
  741.9 200.1 %reduce-scatter.9.cloned.1.call-start = ((), (), s32[]{:S(2)}) async-start(), calls=%async_computation.9 | async-start | bytes 3932160 | tf_op jit(solution)/shard_map/reduce_scatter | solution.py:238
  805.0 6.1 copy-start.8
  805.0 6.1 copy-start.19
  868.6 8.8 copy-start.18
  877.4 1.8 copy-start.10
  877.4 2.0 copy-start.14
  877.4 2.0 copy-start.20
  882.9 128.6 %all-gather.11.cloned.1.call-start = ((), (), s32[]{:S(2)}) async-start(), calls=%async_computation.10 | async-start | bytes 3932160 | tf_op jit(solution)/shard_map/all_gather | solution.py:247
  944.7 9.3 copy-start.38
  947.8 736.5 %all-reduce.8.cloned.1.call-start = ((), (), s32[]{:S(2)}) async-start(), calls=%async_computation.12 | async-start | bytes 14155776 | tf_op jit(solution)/shard_map/psum | solution.py:279
  948.1 5.8 copy-start.9
  948.1 5.8 copy-start.11
  953.9 3.0 copy-start.45
  953.9 3.3 copy-start.48
  957.2 54.3 %copy-start.29 = (bf16[192,768]{1,0:T(8,128)(2,1)S(1)}, bf16[192,768]{1,0:T(8,128)(2,1)}, u32[]{:S(2)}) copy-start(bf16[192,768]{1,0:T(8,128)(2,1)} %param.28) | copy-start | bytes 884740
  1015.4 4.3 copy-start.2
  1054.7 5.1 copy-start.3
  1187.5 5.1 copy-start.3
  1321.1 5.1 copy-start.3
  1455.0 5.1 copy-start.3
  1561.9 2.1 copy-start.4
  1563.8 2.4 copy-start.44
  1566.2 3.3 copy-start.16
  1568.2 1.6 copy-start.13
  1571.4 175.7 %reduce-scatter.11.cloned.1.call-start = ((), (), s32[]{:S(2)}) async-start(), calls=%async_computation.11 | async-start | bytes 3932160 | tf_op jit(solution)/shard_map/reduce_scatter | solution.py:268
  1576.7 1.7 copy-start.49
  1576.7 233.9 %reduce-scatter.7.cloned.1.call-start = ((), (), s32[]{:S(2)}) async-start(), calls=%async_computation.7 | async-start | bytes 3932160 | tf_op jit(solution)/shard_map/reduce_scatter | solution.py:218
  1684.3 4.0 copy-start.23
  1684.4 4.0 copy-start.24
  1684.4 5.2 copy-start.17
  1688.3 2.8 copy-start.22
  1688.4 3.7 copy-start.21
  1689.6 57.5 %copy-start.6 = (bf16[512,768]{1,0:T(8,128)(2,1)S(1)}, bf16[512,768]{1,0:T(8,128)(2,1)}, u32[]{:S(2)}) copy-start(bf16[512,768]{1,0:T(8,128)(2,1)} %param.21) | copy-start | bytes 2359300
  1689.6 57.5 %copy-start.35 = (f32[768]{0:T(1024)S(1)}, f32[768]{0:T(1024)}, u32[]{:S(2)}) copy-start(f32[768]{0:T(1024)} %param.33) | copy-start | bytes 9220
  1689.6 57.5 %copy-start.37 = (f32[512]{0:T(512)S(1)}, f32[512]{0:T(512)}, u32[]{:S(2)}) copy-start(f32[512]{0:T(512)} %copy-done.36) | copy-start | bytes 6148
  1689.6 59.4 %copy-start.42 = (f32[768]{0:T(1024)S(1)}, f32[768]{0:T(1024)}, u32[]{:S(2)}) copy-start(f32[768]{0:T(1024)} %get-tuple-element.584) | copy-start | bytes 9220
  1689.6 104.0 %copy-start.43 = (f32[7]{0:T(128)S(1)}, f32[7]{0:T(128)}, u32[]{:S(2)}) copy-start(f32[7]{0:T(128)} %constant.315) | copy-start | bytes 88
  1689.6 106.5 %copy-start.41 = (f32[512]{0:T(512)S(1)}, f32[512]{0:T(512)}, u32[]{:S(2)}) copy-start(f32[512]{0:T(512)} %copy-done.40) | copy-start | bytes 6148
  1689.6 121.0 %copy-start.7 = (bf16[512,768]{1,0:T(8,128)(2,1)S(1)}, bf16[512,768]{1,0:T(8,128)(2,1)}, u32[]{:S(2)}) copy-start(bf16[512,768]{1,0:T(8,128)(2,1)} %reduce-scatter.5.cloned.1.call-done) | copy-start | bytes 2359300
  1689.7 121.0 %copy-start.15 = (bf16[512,768]{1,0:T(8,128)(2,1)S(1)}, bf16[512,768]{1,0:T(8,128)(2,1)}, u32[]{:S(2)}) copy-start(bf16[512,768]{1,0:T(8,128)(2,1)} %param.22) | copy-start | bytes 2359300
  1689.7 121.0 %copy-start.32 = (f32[768]{0:T(1024)S(1)}, f32[768]{0:T(1024)}, u32[]{:S(2)}) copy-start(f32[768]{0:T(1024)} %param.34) | copy-start | bytes 9220
  1689.7 121.0 %copy-start.34 = (f32[512]{0:T(512)S(1)}, f32[512]{0:T(512)}, u32[]{:S(2)}) copy-start(f32[512]{0:T(512)} %copy-done.33) | copy-start | bytes 6148
  1689.7 121.0 %copy-start.39 = (f32[512]{0:T(512)S(1)}, f32[512]{0:T(512)}, u32[]{:S(2)}) copy-start(f32[512]{0:T(512)} %copy-done.38) | copy-start | bytes 6148
Sparse Core Ops, SparseCore 0:
  12.3 66.1 all-gather.4
  674.5 62.9 reduce-scatter.4
  741.4 63.4 all-gather.6
  806.4 62.1 all-gather.8
  883.0 58.8 reduce-scatter.8
  947.9 63.5 all-gather.10
  1571.5 112.7 all-reduce.7
  1686.6 60.3 reduce-scatter.10
  1749.4 61.1 reduce-scatter.6
where the time goes:
time: 1840 us; the launch traced here: 1820 us
  local copies, waits for them, and re-layouts  879 us (48%)
  waiting for transfers between devices  460 us (25%)
  matrix products  266 us (14%)
  other arithmetic  115 us (6%)
  blocking collectives  44.6 us (2%)
  loops' own time  40.5 us (2%)
    while x32, local copies, waits for them, and re-layouts  440 us
    gather x8, local copies, waits for them, and re-layouts, bucket_onehot(): kind_ids = buckets[jnp.clip(offsets, 0, 2 * limit - 2)]  109 us
    psum x1, waiting for transfers between devices, on_device(): lax.psum((grad_w_query, grad_w_key, grad_w_value, grad_w_out, grad_w_gate...  102 us
    reshape x4, local copies, waits for them, and re-layouts, spread_diagonals(): return sheared.reshape(head_count, height, span - 1)[:, :, :row_width]  92.4 us
    reshape x4, local copies, waits for them, and re-layouts, sum_diagonals(): sheared = padded.reshape(head_count, height, span + 1)[:, :, 1:span]  87.6 us
    dot_general x8, matrix products, block_scores(): jnp.einsum('hqd,hkd->hqk', queries, key_rows, preferred_element_type=jnp....  80.1 us
    reduce_scatter x1, waiting for transfers between devices, on_device(): lax.psum_scatter(jnp.dot(context, w_out, preferred_element_type=jnp.float...  63.1 us
    all_gather x1, waiting for transfers between devices, on_device(): rows_two = lax.all_gather(normed_two, 'mp', axis=0, tiled=True)  62.8 us
  transfers between devices with their start and end apart: 9, of which 8 were waited for; matrix products, arithmetic and copies ran while one was open for 34% of the time, Pallas kernels for 0%

commit v1 on v0

v1 whole, which is shorter than its diff:
```python
import functools

import jax
import jax.numpy as jnp
from jax import lax
from jax.experimental import pallas as pl
from jax.experimental.pallas import tpu as pltpu
from jax.sharding import PartitionSpec as P

NEG = -1e9
LANES = 128

def strip_sizes(limit, tq):
    reach = -(-limit // LANES)
    nq = tq // LANES
    off = LANES * (reach + nq)
    return reach, off, off + LANES * reach + tq

def bucket_hot(buckets, count, tq):
    limit = (buckets.shape[0] + 1) // 2
    _, off, width = strip_sizes(limit, tq)
    back = lax.rev(buckets, (0,))
    shift = off - (limit - 1)
    left = jnp.broadcast_to(back[:1], (shift,))
    right = jnp.broadcast_to(back[-1:], (width - shift - back.shape[0],))
    kinds = jnp.concatenate([left, back, right])
    return (kinds[:, None] == jnp.arange(count, dtype=jnp.int32)[None, :]).astype(jnp.float32)

def ends_list(lens_ref, rows_dev, count):
    total = jnp.int32(0)
    ends = []
    for r in range(rows_dev):
        for c in range(count):
            total = total + lens_ref[r, c]
            ends.append(total)
    return ends

def segment_of(place, ends, count):
    seg = jnp.zeros_like(place)
    pad = jnp.zeros_like(place)
    for n, end in enumerate(ends):
        past = place >= end
        seg = seg + jnp.where(past, 1, 0)
        if n % count == count - 2:
            pad = pad + jnp.where(past, 1, 0)
        if n % count == count - 1:
            pad = pad - jnp.where(past, 1, 0)
    return jnp.where(pad > 0, place + 4096, seg)

def key_range(first, last, ends, count, low_end, high_end, tk):
    low = jnp.int32(0)
    high = ends[-1]
    for n, end in enumerate(ends):
        is_pad_next = n % count == count - 2
        low = jnp.where(first >= end, jnp.maximum(low, first if is_pad_next else end), low)
    for n in range(len(ends) - 1, -1, -1):
        is_pad = n % count == count - 1
        high = jnp.where(last < ends[n], (last + 1) if is_pad else ends[n], high)
    low = (low // LANES) * LANES
    steps = (high - low + tk - 1) // tk
    low = jnp.minimum(low, high_end - steps * tk)
    return pl.multiple_of(low, LANES), steps

def window(place_ref, own, total, limit):
    first = place_ref[0]
    radius = -(-(limit - 1) // own)
    return jnp.maximum(first - radius * own, 0), jnp.minimum(first + (radius + 1) * own, total)

def build_strip(strip, table_ref, hh, width):
    row = table_ref[0, hh : hh + 1, :]
    strip[hh] = pltpu.roll(jnp.broadcast_to(row, (LANES, width)), 0, 1, stride=1, stride_axis=0)

def fill_segments(kseg, ends, count, total):
    def one(n, _):
        at = pl.multiple_of(n * 256, 256)
        place = at + lax.broadcasted_iota(jnp.int32, (256, LANES), 0)
        kseg[pl.ds(at, 256), :] = segment_of(place, ends, count)
        return 0
    lax.fori_loop(0, total // 256, one, 0)

def tile_lanes(x, n):
    return x if n == 1 else jnp.concatenate([x] * n, axis=1)

def lane_start(ks, q_at, g, reach, off, nq):
    d = (ks - q_at) // LANES + g
    return pl.multiple_of(off - LANES * jnp.clip(d, -reach, reach + nq - 1), LANES)

def fwd_kernel(cfg, lens_ref, place_ref, table_ref, q_ref, k_ref, vt_ref, ctx_ref, lse_ref, strip, kseg):
    tq, tk, limit, rows_dev, count, own, total = cfg
    reach, off, width = strip_sizes(limit, tq)
    nq = tq // LANES
    ends = ends_list(lens_ref, rows_dev, count)
    @pl.when(pl.program_id(0) == 0)
    def _():
        fill_segments(kseg, ends, count, total)
    for hh in range(2):
        build_strip(strip, table_ref, hh, width)
    w_low, w_high = window(place_ref, own, total, limit)
    lane = lax.broadcasted_iota(jnp.int32, (tq, LANES), 1)
    for qt in range(own // tq):
        q_at = place_ref[0] + qt * tq
        q2 = q_ref[qt * tq : (qt + 1) * tq, :]
        halves = [jnp.where((lane < 64) == (hh == 0), q2, jnp.zeros_like(q2)) for hh in range(2)]
        qseg = segment_of(q_at + lax.broadcasted_iota(jnp.int32, (1, tq), 1), ends, count)
        low, steps = key_range(q_at, q_at + tq - 1, ends, count, w_low, w_high, tk)
        def step(c, carry):
            ks = pl.multiple_of(low + c * tk, LANES)
            kc = k_ref[pl.ds(ks, tk), :]
            same = tile_lanes(kseg[pl.ds(ks, tk), :], nq) == qseg
            out = []
            for hh in range(2):
                top, tot, acc = carry[hh]
                s = lax.dot_general(kc, halves[hh], (((1,), (1,)), ((), ())), preferred_element_type=jnp.float32)
                bias = jnp.concatenate([strip[hh, :, pl.ds(lane_start(ks, q_at, g, reach, off, nq), tq)] for g in range(tk // LANES)], axis=0)
                s = jnp.where(same, s + bias, NEG)
                new = jnp.maximum(top, jnp.max(s, axis=0, keepdims=True))
                p = jnp.exp(s - new)
                fade = jnp.exp(top - new)
                tot = tot * fade + jnp.sum(p, axis=0, keepdims=True)
                acc = acc * fade + jnp.dot(vt_ref[hh * 64 : hh * 64 + 64, pl.ds(ks, tk)], p.astype(jnp.bfloat16), preferred_element_type=jnp.float32)
                out.append((new, tot, acc))
            return tuple(out)
        zero = (jnp.full((1, tq), 2 * NEG, jnp.float32), jnp.zeros((1, tq), jnp.float32), jnp.zeros((64, tq), jnp.float32))
        res = lax.fori_loop(0, steps, step, (zero, zero))
        both = jnp.concatenate([res[hh][2] / res[hh][1] for hh in range(2)], axis=0)
        ctx_ref[qt * tq : (qt + 1) * tq, :] = both.T.astype(jnp.bfloat16)
        for hh in range(2):
            lse_ref[0, hh : hh + 1, qt * tq : (qt + 1) * tq] = res[hh][0] + jnp.log(res[hh][1])

def attend(lengths, place, table, q, k, vt, limit, tq=256, tk=256):
    own, inner = q.shape
    total = k.shape[0]
    pairs = inner // LANES
    rows_dev, count = lengths.shape
    width = strip_sizes(limit, tq)[2]
    cfg = (tq, tk, limit, rows_dev, count, own, total)
    smem = pl.BlockSpec(memory_space=pltpu.SMEM)
    return pl.pallas_call(
        functools.partial(fwd_kernel, cfg),
        grid=(pairs,),
        in_specs=[smem, smem,
            pl.BlockSpec((1, 2, width), lambda p: (p, 0, 0)),
            pl.BlockSpec((own, LANES), lambda p: (0, p)),
            pl.BlockSpec((total, LANES), lambda p: (0, p)),
            pl.BlockSpec((LANES, total), lambda p: (p, 0))],
        out_specs=[pl.BlockSpec((own, LANES), lambda p: (0, p)),
                   pl.BlockSpec((1, 2, own), lambda p: (p, 0, 0))],
        out_shape=[jax.ShapeDtypeStruct((own, inner), jnp.bfloat16), jax.ShapeDtypeStruct((pairs, 2, own), jnp.float32)],
        scratch_shapes=[pltpu.VMEM((2, LANES, width), jnp.float32), pltpu.VMEM((total, LANES), jnp.int32)],
        compiler_params=pltpu.CompilerParams(vmem_limit_bytes=56 * 2**20),
        name="attend",
    )(lengths, place, table, q, k, vt)

def bwd_kernel(cfg, lens_ref, place_ref, table_ref, q_ref, k_ref, kt_ref, v_ref, ctx_ref, do_ref, lse_ref,
               dq_ref, dk_ref, dv_ref, diag_ref, strip, dstrip, kseg, dk_acc, dv_acc):
    tq, tk, limit, rows_dev, count, own, total = cfg
    reach, off, width = strip_sizes(limit, tq)
    nq = tq // LANES
    ends = ends_list(lens_ref, rows_dev, count)
    @pl.when(pl.program_id(0) == 0)
    def _():
        fill_segments(kseg, ends, count, total)
    for hh in range(2):
        build_strip(strip, table_ref, hh, width)
    dstrip[...] = jnp.zeros_like(dstrip)
    dk_acc[...] = jnp.zeros_like(dk_acc)
    dv_acc[...] = jnp.zeros_like(dv_acc)
    w_low, w_high = window(place_ref, own, total, limit)
    lane = lax.broadcasted_iota(jnp.int32, (tq, LANES), 1)
    for qt in range(own // tq):
        rows = slice(qt * tq, (qt + 1) * tq)
        q_at = place_ref[0] + qt * tq
        q2 = q_ref[rows, :]
        do2 = do_ref[rows, :]
        prod = (do2.astype(jnp.float32) * ctx_ref[rows, :].astype(jnp.float32)).T
        q_half = [jnp.where((lane < 64) == (hh == 0), q2, jnp.zeros_like(q2)) for hh in range(2)]
        do_half = [jnp.where((lane < 64) == (hh == 0), do2, jnp.zeros_like(do2)) for hh in range(2)]
        delta = [jnp.sum(prod[hh * 64 : hh * 64 + 64], axis=0, keepdims=True) for hh in range(2)]
        lse = [lse_ref[0, hh : hh + 1, rows] for hh in range(2)]
        qseg = segment_of(q_at + lax.broadcasted_iota(jnp.int32, (1, tq), 1), ends, count)
        low, steps = key_range(q_at, q_at + tq - 1, ends, count, w_low, w_high, tk)
        def step(c, carry):
            ks = pl.multiple_of(low + c * tk, LANES)
            kc = k_ref[pl.ds(ks, tk), :]
            vc = v_ref[pl.ds(ks, tk), :]
            same = tile_lanes(kseg[pl.ds(ks, tk), :], nq) == qseg
            out = []
            dk_part = dv_part = None
            for hh in range(2):
                s = lax.dot_general(kc, q_half[hh], (((1,), (1,)), ((), ())), preferred_element_type=jnp.float32)
                starts = [lane_start(ks, q_at, g, reach, off, nq) for g in range(tk // LANES)]
                bias = jnp.concatenate([strip[hh, :, pl.ds(at, tq)] for at in starts], axis=0)
                p = jnp.exp(jnp.where(same, s + (bias - lse[hh]), NEG))
                dp = lax.dot_general(vc, do_half[hh], (((1,), (1,)), ((), ())), preferred_element_type=jnp.float32)
                ds = p * (dp - delta[hh])
                for g, at in enumerate(starts):
                    dstrip[hh, :, pl.ds(at, tq)] += ds[g * LANES : (g + 1) * LANES, :]
                pb = p.astype(jnp.bfloat16)
                dsb = ds.astype(jnp.bfloat16)
                dv_one = jnp.dot(pb, do_half[hh], preferred_element_type=jnp.float32)
                dk_one = jnp.dot(dsb, q_half[hh], preferred_element_type=jnp.float32)
                dv_part = dv_one if dv_part is None else dv_part + dv_one
                dk_part = dk_one if dk_part is None else dk_part + dk_one
                out.append(carry[hh] + jnp.dot(kt_ref[hh * 64 : hh * 64 + 64, pl.ds(ks, tk)], dsb, preferred_element_type=jnp.float32))
            dv_acc[pl.ds(ks, tk), :] += dv_part
            dk_acc[pl.ds(ks, tk), :] += dk_part
            return tuple(out)
        zero = jnp.zeros((64, tq), jnp.float32)
        res = lax.fori_loop(0, steps, step, (zero, zero))
        dq_ref[rows, :] = jnp.concatenate(res, axis=0).T.astype(jnp.bfloat16)
    dk_ref[...] = dk_acc[...].astype(jnp.bfloat16)
    dv_ref[...] = dv_acc[...].astype(jnp.bfloat16)
    for hh in range(2):
        eight = dstrip[hh, 0:8, :]
        for g in range(1, LANES // 8):
            eight = eight + pltpu.roll(dstrip[hh, 8 * g : 8 * g + 8, :], width - 8 * g, 1)
        flat = eight[0:1, :]
        for r in range(1, 8):
            flat = flat + pltpu.roll(eight[r : r + 1, :], width - r, 1)
        diag_ref[0, hh : hh + 1, :] = flat

def attend_back(lengths, place, table, q, k, kt, v, ctx, do, lse, limit, tq=256, tk=256):
    own, inner = q.shape
    total = k.shape[0]
    pairs = inner // LANES
    rows_dev, count = lengths.shape
    width = strip_sizes(limit, tq)[2]
    cfg = (tq, tk, limit, rows_dev, count, own, total)
    smem = pl.BlockSpec(memory_space=pltpu.SMEM)
    tall = pl.BlockSpec((total, LANES), lambda p: (0, p))
    short = pl.BlockSpec((own, LANES), lambda p: (0, p))
    return pl.pallas_call(
        functools.partial(bwd_kernel, cfg),
        grid=(pairs,),
        in_specs=[smem, smem,
            pl.BlockSpec((1, 2, width), lambda p: (p, 0, 0)),
            short, tall, pl.BlockSpec((LANES, total), lambda p: (p, 0)), tall, short, short,
            pl.BlockSpec((1, 2, own), lambda p: (p, 0, 0))],
        out_specs=[short, tall, tall, pl.BlockSpec((1, 2, width), lambda p: (p, 0, 0))],
        out_shape=[jax.ShapeDtypeStruct((own, inner), jnp.bfloat16), jax.ShapeDtypeStruct((total, inner), jnp.bfloat16),
                   jax.ShapeDtypeStruct((total, inner), jnp.bfloat16), jax.ShapeDtypeStruct((pairs, 2, width), jnp.float32)],
        scratch_shapes=[pltpu.VMEM((2, LANES, width), jnp.float32), pltpu.VMEM((2, LANES, width), jnp.float32), pltpu.VMEM((total, LANES), jnp.int32),
                        pltpu.VMEM((total, LANES), jnp.float32), pltpu.VMEM((total, LANES), jnp.float32)],
        compiler_params=pltpu.CompilerParams(vmem_limit_bytes=56 * 2**20),
        name="attend_back",
    )(lengths, place, table, q, k, kt, v, ctx, do, lse)


MESH = pl.DeviceIdType.MESH
GROUP = 8


def flip(index, bit):
    return index + bit * (1 - 2 * ((index // bit) % 2))


class Links:
    def __init__(self, send_sems, recv_sems, batch, place):
        self.send_sems, self.recv_sems = send_sems, recv_sems
        self.batch, self.place = batch, place
        self.slots = {}
        self.sent = []

    def slot(self, key):
        return self.slots.setdefault(key, len(self.slots))

    def copy(self, key, src, dst, target):
        n = self.slot(key)
        return pltpu.make_async_remote_copy(
            src_ref=src, dst_ref=dst, send_sem=self.send_sems.at[n], recv_sem=self.recv_sems.at[n],
            device_id=target, device_id_type=MESH)

    def send(self, key, src, dst, target, when=None):
        def go():
            self.copy(key, src, dst, target).start()
        self.sent.append((key, src, dst, target, when))
        if when is None:
            go()
        else:
            pl.when(when)(go)

    def take(self, key, dst, when=None, then=None):
        def go():
            self.copy(key, dst, dst, (self.batch, self.place)).wait_recv()
            if then is not None:
                then()
        if when is None:
            go()
        else:
            pl.when(when)(go)

    def drain(self):
        for key, src, dst, target, when in self.sent:
            def go():
                self.copy(key, src, dst, target).wait_send()
            if when is None:
                go()
            else:
                pl.when(when)(go)


def greet(batch, place, count):
    bar = pltpu.get_barrier_semaphore()
    for bit in (1, 2, 4):
        pl.semaphore_signal(bar, inc=1, device_id=(flip(batch, bit), place), device_id_type=MESH)
    for way in range(1 - count, count):
        if way != 0:
            @pl.when((place + way >= 0) & (place + way < count))
            def _():
                pl.semaphore_signal(bar, inc=1, device_id=(batch, place + way), device_id_type=MESH)
    pl.semaphore_wait(bar, 3 + count - 1)


def both(a, b):
    return a if b is None else (b if a is None else a & b)


class PlaneGather:
    def __init__(self, links, key, view, ref, sub, when=None):
        self.l, self.key, self.view, self.ref, self.sub, self.when = links, key, view, ref, sub, when

    def put(self, path, sub, half, bit):
        region = self.view(self.ref, sub, half)
        self.l.send((self.key, path), region, region, (flip(self.l.batch, bit), self.l.place), self.when)

    def start(self):
        self.put("x", self.sub, None, 2)
        self.put("y", self.sub, None, 4)
        self.put("c", self.sub, None, 1)

    def middle(self):
        sub = self.sub
        self.l.take((self.key, "x"), self.view(self.ref, flip(sub, 2), None), self.when)
        self.put("xy", flip(sub, 2), 0, 4)
        self.put("xc", flip(sub, 2), None, 1)
        self.l.take((self.key, "y"), self.view(self.ref, flip(sub, 4), None), self.when)
        self.put("yx", flip(sub, 4), 1, 2)
        self.put("yc", flip(sub, 4), None, 1)

    def far(self):
        sub = self.sub
        diagonal = flip(flip(sub, 2), 4)
        self.l.take((self.key, "xy"), self.view(self.ref, diagonal, 0), self.when)
        self.put("0c", diagonal, 0, 1)
        self.l.take((self.key, "yx"), self.view(self.ref, diagonal, 1), self.when)
        self.put("1c", diagonal, 1, 1)

    def end(self):
        sub = flip(self.sub, 1)
        diagonal = flip(flip(sub, 2), 4)
        self.l.take((self.key, "c"), self.view(self.ref, sub, None), self.when)
        self.l.take((self.key, "xc"), self.view(self.ref, flip(sub, 2), None), self.when)
        self.l.take((self.key, "yc"), self.view(self.ref, flip(sub, 4), None), self.when)
        self.l.take((self.key, "0c"), self.view(self.ref, diagonal, 0), self.when)
        self.l.take((self.key, "1c"), self.view(self.ref, diagonal, 1), self.when)


def half_rows(half, rows):
    return pl.ds(0, rows) if half is None else pl.ds(half * (rows // 2), rows // 2)


PIECES = 4


def gather_kernel(count, radius, x_ref, wa_ref, wf_ref, xs_ref, was_ref, wfs_ref, blank, send_sems, recv_sems, local_sems):
    batch, place = lax.axis_index("batch"), lax.axis_index("mp")
    sub = batch % GROUP
    links = Links(send_sems, recv_sems, batch, place)
    own = x_ref.shape[0]
    rows_a = wa_ref.shape[2]
    rows_f = wf_ref.shape[2]
    step = own // PIECES
    local = [
        pltpu.make_async_copy(wa_ref, was_ref.at[:, place], local_sems.at[0]),
        pltpu.make_async_copy(wf_ref, wfs_ref.at[:, place], local_sems.at[1]),
        pltpu.make_async_copy(x_ref, xs_ref.at[place], local_sems.at[2]),
    ]
    for one in local:
        one.start()
    blank[...] = jnp.zeros_like(blank)
    outside = []
    for n in range(count):
        far = (n - place > radius) | (place - n > radius)
        outside.append((far, pltpu.make_async_copy(blank, xs_ref.at[n], local_sems.at[3 + n])))
    for far, one in outside:
        pl.when(far)(one.start)
    greet(batch, place, count)

    def view_a(mm):
        return lambda ref, s, half: ref.at[s // 2, mm, s % 2, half_rows(half, rows_a)]

    def view_f(mm):
        return lambda ref, s, half: ref.at[:, mm, s, half_rows(half, rows_f)]

    def inside(n):
        return (n >= 0) & (n < count)

    for way in (1, -1):
        ok = inside(place + way)
        target = (batch, place + way)
        links.send(("a", way, 1), wa_ref.at[sub // 2, sub % 2], view_a(place)(was_ref, sub, None), target, ok)
        links.send(("f", way, 1), wf_ref.at[:, sub], view_f(place)(wfs_ref, sub, None), target, ok)
    for way in (1, -1):
        ok = inside(place + way)
        target = (batch, place + way)
        for p in range(PIECES):
            rows = pl.ds(p * step, step)
            links.send(("x", way, 1, p), x_ref.at[rows], xs_ref.at[place, rows], target, ok)

    gathers = {}

    def weights_arrive(kind, dist):
        for way in (1, -1):
            source = place - way * dist
            ok = inside(source)
            view, ref = (view_a(source), was_ref) if kind == "a" else (view_f(source), wfs_ref)
            region = view(ref, sub, None)
            links.take((kind, way, dist), region, ok)
            if dist < count - 1:
                links.send((kind, way, dist + 1), region, region, (batch, place + way), ok & inside(place + way))
            gather = PlaneGather(links, ("g", kind, way, dist), view, ref, sub, ok)
            gather.start()
            gathers[kind, way, dist] = gather

    def x_arrive(dist, p):
        for way in (1, -1):
            source = place - way * dist
            ok = inside(source)
            region = xs_ref.at[source, pl.ds(p * step, step)]
            links.take(("x", way, dist, p), region, ok)
            if dist < radius:
                links.send(("x", way, dist + 1, p), region, region, (batch, place + way), ok & inside(place + way))

    def stage(name, kind, dist):
        for way in (1, -1):
            getattr(gathers[kind, way, dist], name)()

    dists = range(1, count)
    for d in dists:
        weights_arrive("a", d)
    weights_arrive("f", 1)
    for d in dists:
        stage("middle", "a", d)
    for p in range(PIECES):
        x_arrive(1, p)
        if p + 2 < count:
            weights_arrive("f", p + 2)
        if p == 1:
            stage("middle", "f", 1)
    for d in dists:
        stage("far", "a", d)
    for d in range(2, count):
        stage("middle", "f", d)
    for d in dists:
        stage("far", "f", d)
    for r in range(2, radius + 1):
        for p in range(PIECES):
            x_arrive(r, p)
    for kind in ("a", "f"):
        for d in dists:
            stage("end", kind, d)
    links.drain()
    for one in local:
        one.wait()
    for far, one in outside:
        pl.when(far)(one.wait)


def gather(x, wa, wf, count, radius):
    own, width = x.shape
    return pl.pallas_call(
        functools.partial(gather_kernel, count, radius),
        in_specs=[pl.BlockSpec(memory_space=pl.ANY)] * 3,
        out_specs=[pl.BlockSpec(memory_space=pl.ANY)] * 3,
        out_shape=[
            jax.ShapeDtypeStruct((count, own, width), x.dtype),
            jax.ShapeDtypeStruct((wa.shape[0], count) + wa.shape[1:], wa.dtype),
            jax.ShapeDtypeStruct((wf.shape[0], count) + wf.shape[1:], wf.dtype),
        ],
        scratch_shapes=[
            pltpu.VMEM((own, width), x.dtype),
            pltpu.SemaphoreType.DMA((160,)),
            pltpu.SemaphoreType.DMA((160,)),
            pltpu.SemaphoreType.DMA((8 + count,)),
        ],
        compiler_params=pltpu.CompilerParams(collective_id=1, has_side_effects=True, vmem_limit_bytes=32 * 2**20),
        name="gather",
    )(x, wa, wf)


def add_blocks(count, target, extra):
    def one(n, _):
        t, e = target(n), extra(n)
        t[...] = t[...] + e[...]
        return 0
    lax.fori_loop(0, count, one, 0)


def reduce_kernel(count, radius, scale, final, gx_ref, ga_ref, gg_ref, gu_ref, gd_ref, small_ref,
                  gn_ref, oa_ref, of_ref, side_ref, total_ref,
                  keep_a, got_a1, got_ax, got_ay, got_ay2, got_ax2, keep_f, got_f1, got_fx, got_fy, got_fy2, got_fx2,
                  from_a, from_f, full_a, full_f, got_x, tiny, tiny_z, side_z, send_sems, recv_sems, local_sems):
    batch, place = lax.axis_index("batch"), lax.axis_index("mp")
    sub = batch % GROUP
    core, xx, yy = sub % 2, (sub // 2) % 2, sub // 4
    links = Links(send_sems, recv_sems, batch, place)
    gf_refs = [gg_ref, gu_ref, gd_ref]
    rows_a, rows_f = keep_a.shape[3], keep_f.shape[4]
    ha, hf = rows_a // 2, rows_f // 2
    own = gn_ref.shape[0]
    step = own // PIECES

    def inside(n):
        return (n >= 0) & (n < count)

    sibling, x_near, y_near = [(flip(batch, bit), place) for bit in (1, 2, 4)]
    local_f = [pltpu.make_async_copy(gf_refs[t].at[:, :, :, core], keep_f.at[t], local_sems.at[t]) for t in range(3)]
    local_a = pltpu.make_async_copy(ga_ref.at[:, :, :, core], keep_a, local_sems.at[3])
    for one in local_f + [local_a]:
        one.start()
    greet(batch, place, count)
    for t in range(3):
        links.send(("f1", t), gf_refs[t].at[:, :, :, 1 - core], got_f1.at[t], sibling)
    links.send(("a1",), ga_ref.at[:, :, :, 1 - core], got_a1, sibling)
    for way in (1, -1):
        for p in range(PIECES):
            rows = pl.ds(p * step, step)
            dest = place + way * radius
            links.send(("x", way, radius, p), gx_ref.at[jnp.clip(dest, 0, count - 1), rows],
                       got_x.at[0 if way > 0 else 1, radius - 1, rows], (batch, place + way), inside(dest))
    links.send(("s", 0), small_ref, tiny.at[1], sibling)

    def start_a(t):
        if t == "a":
            links.send(("ax",), keep_a.at[:, 1 - xx, :, pl.ds(0, ha)], got_ax, x_near)
            links.send(("ay",), keep_a.at[1 - yy, :, :, pl.ds(ha, ha)], got_ay, y_near)
        else:
            links.send(("fx", t), keep_f.at[t, :, :, 1 - xx, pl.ds(0, hf)], got_fx.at[t], x_near)
            links.send(("fy", t), keep_f.at[t, :, 1 - yy, :, pl.ds(hf, hf)], got_fy.at[t], y_near)

    for t in range(3):
        local_f[t].wait()
        links.take(("f1", t), got_f1.at[t])
        def one(n, _):
            for i in range(2):
                for j in range(2):
                    keep_f[t, n, i, j] = keep_f[t, n, i, j] + got_f1[t, n, i, j]
            return 0
        lax.fori_loop(0, count, one, 0)
        start_a(t)
    local_a.wait()
    links.take(("a1",), got_a1)
    def one_a(n, _):
        for i in range(2):
            for j in range(2):
                keep_a[i, j, n] = keep_a[i, j, n] + got_a1[i, j, n]
        return 0
    lax.fori_loop(0, count, one_a, 0)
    start_a("a")

    def tiny_step(n):
        links.take(("s", n), tiny.at[2 * n + 1])
        before = small_ref if n == 0 else tiny.at[2 * n]
        tiny[2 * n + 2] = before[...] + tiny[2 * n + 1]
        if n < 2:
            links.send(("s", n + 1), tiny.at[2 * n + 2], tiny.at[2 * n + 3], (flip(batch, 2 << n), place))
        else:
            tiny_z[place] = tiny[6]
            for d in range(1, count):
                for way in (1, -1):
                    links.send(("sz", way, d), tiny.at[6], tiny_z.at[place], (batch, place + way * d), inside(place + way * d))

    tiny_step(0)

    def x_step(level, p):
        rows = pl.ds(p * step, step)
        for side, way in ((0, 1), (1, -1)):
            dest = place + way * (level - 1)
            ok = inside(place - way) & inside(dest)
            def add():
                got_x[side, level - 1, rows] = got_x[side, level - 1, rows] + gx_ref[dest, rows]
            links.take(("x", way, level, p), got_x.at[side, level - 1, rows], ok, add if level > 1 else None)
            if level > 1:
                ok2 = inside(place - way) & inside(dest)
                links.send(("x", way, level - 1, p), got_x.at[side, level - 1, rows], got_x.at[side, level - 2, rows],
                           (batch, place + way), ok2)
                links.send(("x0", way, level - 1, p), gx_ref.at[jnp.clip(dest, 0, count - 1), rows], got_x.at[side, level - 2, rows],
                           (batch, place + way), jnp.logical_not(inside(place - way)) & inside(dest))

    for level in range(radius, 1, -1):
        for p in range(PIECES):
            x_step(level, p)
    tiny_step(1)

    def middle(t):
        if t == "a":
            links.take(("ax",), got_ax)
            links.take(("ay",), got_ay)
            def one(n, _):
                for i in range(2):
                    keep_a[i, xx, n, pl.ds(0, ha)] = keep_a[i, xx, n, pl.ds(0, ha)] + got_ax[i, n]
                    keep_a[yy, i, n, pl.ds(ha, ha)] = keep_a[yy, i, n, pl.ds(ha, ha)] + got_ay[i, n]
                return 0
            lax.fori_loop(0, count, one, 0)
            links.send(("ay2",), keep_a.at[1 - yy, xx, :, pl.ds(0, ha)], got_ay2, y_near)
            links.send(("ax2",), keep_a.at[yy, 1 - xx, :, pl.ds(ha, ha)], got_ax2, x_near)
        else:
            links.take(("fx", t), got_fx.at[t])
            links.take(("fy", t), got_fy.at[t])
            def one(n, _):
                for i in range(2):
                    keep_f[t, n, i, xx, pl.ds(0, hf)] = keep_f[t, n, i, xx, pl.ds(0, hf)] + got_fx[t, n, i]
                    keep_f[t, n, yy, i, pl.ds(hf, hf)] = keep_f[t, n, yy, i, pl.ds(hf, hf)] + got_fy[t, n, i]
                return 0
            lax.fori_loop(0, count, one, 0)
            links.send(("fy2", t), keep_f.at[t, :, 1 - yy, xx, pl.ds(0, hf)], got_fy2.at[t], y_near)
            links.send(("fx2", t), keep_f.at[t, :, yy, 1 - xx, pl.ds(hf, hf)], got_fx2.at[t], x_near)

    def unit(t, n):
        return keep_a.at[yy, xx, n] if t == "a" else keep_f.at[t, n, yy, xx]

    def arrived(t, side, n):
        return from_a.at[side, n] if t == "a" else from_f.at[t, side, n]

    def last(t):
        if t == "a":
            links.take(("ay2",), got_ay2)
            links.take(("ax2",), got_ax2)
            def one(n, _):
                keep_a[yy, xx, n, pl.ds(0, ha)] = keep_a[yy, xx, n, pl.ds(0, ha)] + got_ay2[n]
                keep_a[yy, xx, n, pl.ds(ha, ha)] = keep_a[yy, xx, n, pl.ds(ha, ha)] + got_ax2[n]
                return 0
        else:
            links.take(("fy2", t), got_fy2.at[t])
            links.take(("fx2", t), got_fx2.at[t])
            def one(n, _):
                keep_f[t, n, yy, xx, pl.ds(0, hf)] = keep_f[t, n, yy, xx, pl.ds(0, hf)] + got_fy2[t, n]
                keep_f[t, n, yy, xx, pl.ds(hf, hf)] = keep_f[t, n, yy, xx, pl.ds(hf, hf)] + got_fx2[t, n]
                return 0
        lax.fori_loop(0, count, one, 0)

    def line(t, hop):
        for side, way in ((0, 1), (1, -1)):
            for n in (range(count - 1, 0, -1) if way > 0 else range(count - 1)):
                first = place == (0 if way > 0 else count - 1)
                beyond = (n > place) if way > 0 else (n < place)
                here = place == (hop if way > 0 else count - 1 - hop)
                if hop > 0:
                    def add():
                        ref, more = unit(t, n), arrived(t, side, n)
                        ref[...] = ref[...] + more[...]
                    links.take(("z", t, side, n, hop - 1), arrived(t, side, n), here & beyond, add)
                links.send(("z", t, side, n, hop), unit(t, n), arrived(t, side, n), (batch, place + way), here & beyond)

    def view_a(ref, s, half):
        return ref.at[s // 2, s % 2, half_rows(half, rows_a)]

    def view_f(t):
        return lambda ref, s, half: ref.at[t, s, half_rows(half, rows_f)]

    gathers = {}

    def finish(t):
        for side, way in ((0, 1), (1, -1)):
            for hop in range(count - 1):
                def add():
                    ref, more = unit(t, place), arrived(t, side, place)
                    ref[...] = ref[...] + more[...]
                for n in range(count):
                    here = (place == n) & (place == (hop + 1 if way > 0 else count - 2 - hop))
                    if (n == hop + 1) if way > 0 else (n == count - 2 - hop):
                        links.take(("z", t, side, n, hop), arrived(t, side, n), here, add)
        if t == "a":
            view, ref = view_a, full_a
            full_a[sub // 2, sub % 2] = keep_a[yy, xx, place]
        else:
            view, ref = view_f(t), full_f
            full_f[t, sub] = keep_f[t, place, yy, xx]
        gathers[t] = PlaneGather(links, ("g", t), view, ref, sub)
        gathers[t].start()

    order = [0, 1, 2, "a"]
    for t in order:
        middle(t)
    tiny_step(2)
    for t in order:
        last(t)
        line(t, 0)
    for p in range(PIECES):
        for side, way in ((0, 1), (1, -1)):
            rows = pl.ds(p * step, step)
            ok = inside(place - way)
            near = inside(place - 2 * way)
            if radius > 1:
                links.take(("x", way, 1, p), got_x.at[side, 0, rows], ok & near)
                links.take(("x0", way, 1, p), got_x.at[side, 0, rows], ok & jnp.logical_not(near))
            else:
                links.take(("x", way, 1, p), got_x.at[side, 0, rows], ok)
            def fill():
                got_x[side, 0, rows] = jnp.zeros((step, got_x.shape[3]), got_x.dtype)
            pl.when(jnp.logical_not(ok))(fill)
        rows = pl.ds(p * step, step)
        gn_ref[rows, :] = (gx_ref[place, rows].astype(jnp.float32) + got_x[0, 0, rows].astype(jnp.float32)
                           + got_x[1, 0, rows].astype(jnp.float32))
    for hop in range(1, count - 1):
        for t in order:
            line(t, hop)
    for t in order:
        finish(t)
    for d in range(1, count):
        for way in (1, -1):
            links.take(("sz", way, d), tiny_z.at[place - way * d], inside(place - way * d))
    summed = tiny_z[0]
    for n in range(1, count):
        summed = summed + tiny_z[n]
    total_ref[...] = summed
    for name in ("middle", "far", "end"):
        for t in order:
            getattr(gathers[t], name)()

    def scaled(value):
        return value.astype(jnp.float32) * scale if final else value.astype(jnp.float32)

    sums = []
    for s in range(4):
        acc = jnp.zeros((8, full_a.shape[3]), jnp.float32)
        for j in range(2):
            def one(r, acc):
                rows = pl.ds(pl.multiple_of(r * 32, 32), 32)
                value = scaled(full_a[s, j, rows])
                oa_ref[s, j, rows] = value
                sq = value * value
                return acc + sq[0:8] + sq[8:16] + sq[16:24] + sq[24:32]
            acc = lax.fori_loop(0, rows_a // 32, one, acc)
        sums.append(jnp.sum(acc, axis=0, keepdims=True))
    for t in range(3):
        def one(n, acc):
            for r in range(rows_f // 32):
                rows = pl.ds(r * 32, 32)
                value = scaled(full_f[t, n, rows])
                of_ref[t, n, rows] = value
                sq = value * value
                acc = acc + sq[0:8] + sq[8:16] + sq[16:24] + sq[24:32]
            return acc
        sums.append(jnp.sum(lax.fori_loop(0, GROUP, one, jnp.zeros((8, full_a.shape[3]), jnp.float32)), axis=0, keepdims=True))
    sums.append(jnp.zeros_like(sums[0]))
    side_z[place] = jnp.concatenate(sums, axis=0)
    for d in range(1, count):
        for way in (1, -1):
            links.send(("q", way, d), side_z.at[place], side_z.at[place], (batch, place + way * d), inside(place + way * d))
    for d in range(1, count):
        for way in (1, -1):
            links.take(("q", way, d), side_z.at[place - way * d], inside(place - way * d))
    summed = side_z[0]
    for n in range(1, count):
        summed = summed + side_z[n]
    side_ref[...] = summed
    links.drain()


def reduce(gx, ga, gfs, small, count, radius, scale, final):
    _, own, width = gx.shape
    bf = jnp.bfloat16
    ra, rf = ga.shape[4], gfs[0].shape[4]
    vm = pl.BlockSpec(memory_space=pltpu.VMEM)
    hb = pl.BlockSpec(memory_space=pl.ANY)
    V = lambda *s: pltpu.VMEM(s + (width,), bf)
    S = small.shape[0]
    return pl.pallas_call(
        functools.partial(reduce_kernel, count, radius, scale, final),
        in_specs=[vm, hb, hb, hb, hb, vm],
        out_specs=[vm] * 5,
        out_shape=[
            jax.ShapeDtypeStruct((own, width), jnp.float32),
            jax.ShapeDtypeStruct((4, 2, ra, width), jnp.float32),
            jax.ShapeDtypeStruct((3, GROUP, rf, width), jnp.float32),
            jax.ShapeDtypeStruct((8, width), jnp.float32),
            jax.ShapeDtypeStruct((S, width), jnp.float32),
        ],
        scratch_shapes=[
            V(2, 2, count, ra), V(2, 2, count, ra), V(2, count, ra // 2), V(2, count, ra // 2), V(count, ra // 2), V(count, ra // 2),
            V(3, count, 2, 2, rf), V(3, count, 2, 2, rf), V(3, count, 2, rf // 2), V(3, count, 2, rf // 2), V(3, count, rf // 2), V(3, count, rf // 2),
            V(2, count, ra), V(3, 2, count, rf), V(4, 2, ra), V(3, GROUP, rf), V(2, radius, own),
            pltpu.VMEM((7, S, width), jnp.float32), pltpu.VMEM((count, S, width), jnp.float32), pltpu.VMEM((count, 8, width), jnp.float32),
            pltpu.SemaphoreType.DMA((240,)), pltpu.SemaphoreType.DMA((240,)), pltpu.SemaphoreType.DMA((4,)),
        ],
        compiler_params=pltpu.CompilerParams(collective_id=2, has_side_effects=True, vmem_limit_bytes=56 * 2**20),
        name="reduce",
    )(gx, ga, *gfs, small)


EPS = 1e-06
TINY = 1e-30
HIGH = lax.Precision.HIGHEST


def norm_rows(values, gain_vec):
    return values * lax.rsqrt(jnp.mean(values * values, axis=-1, keepdims=True) + EPS) * gain_vec


def mm(a, b, ca, cb):
    return lax.dot_general(a, b, (((ca,), (cb,)), ((), ())), preferred_element_type=jnp.float32)


def on_device(tokens, cotangent, lengths, buckets, w_query, w_key, w_value, w_out, w_gate, w_up, w_down, rel_table, gain_one, gain_two):
    bf = jnp.bfloat16
    count = lax.axis_size("mp")
    batches = lax.axis_size("batch")
    own, width = tokens.shape
    total = own * count
    inner = w_query.shape[1]
    hidden_rows = w_gate.shape[1]
    limit = (buckets.shape[0] + 1) // 2
    radius = min(count - 1, -(-(limit - 1) // own))
    place = jnp.reshape(lax.axis_index("mp") * own, (1,)).astype(jnp.int32)
    kinds = rel_table.shape[0]
    heads = rel_table.shape[1] * count

    wa = jnp.concatenate([w_query.T, w_key.T, w_value.T, w_out], axis=0).reshape(4, 2, inner // 2, width)
    wf = jnp.stack([w_gate.T, w_up.T, w_down]).reshape(3, GROUP, hidden_rows // GROUP, width)
    inputs = tokens.astype(jnp.float32)
    normed_one = norm_rows(inputs, gain_one).astype(bf)
    rel_all = lax.all_gather(rel_table, "mp", axis=1, tiled=True)
    hot = bucket_hot(buckets, kinds, TQ)
    table = jnp.dot(hot, rel_all, precision=HIGH).T.reshape(heads // 2, 2, -1)

    rows_one, wa_all, wf_all = gather(normed_one, wa, wf, count, radius)
    rows_one = rows_one.reshape(total, width)
    wa_all = wa_all.reshape(4, count * inner, width)
    wf_all = wf_all.reshape(3, count * hidden_rows, width)
    wq, wk, wv, wo = [wa_all[n] for n in range(4)]
    wg, wu, wd = [wf_all[n] for n in range(3)]

    q = mm(normed_one, wq, 1, 1).astype(bf)
    k = mm(rows_one, wk, 1, 1).astype(bf)
    kt = mm(wk, rows_one, 1, 1).astype(bf)
    v = mm(rows_one, wv, 1, 1).astype(bf)
    vt = mm(wv, rows_one, 1, 1).astype(bf)
    context, lse = attend(lengths, place, table, q, k, vt, limit, TQ, TK)

    middle = inputs + mm(context, wo, 1, 0)
    normed_two = norm_rows(middle, gain_two).astype(bf)
    gate_pre = mm(normed_two, wg, 1, 1)
    up_proj = mm(normed_two, wu, 1, 1)

    def gated_unit(gate_in, up_in):
        return jax.nn.gelu(gate_in, approximate=True) * up_in

    hidden, unit_back = jax.vjp(gated_unit, gate_pre, up_proj)
    hidden = hidden.astype(bf)
    layer_out = (middle + mm(hidden, wd, 1, 0)).astype(bf)
    grad_gate, grad_up = unit_back(mm(cotangent, wd, 1, 1))
    grad_gate = grad_gate.astype(bf)
    grad_up = grad_up.astype(bf)
    raw_down = mm(hidden, cotangent, 0, 0).astype(bf)
    raw_gate = mm(grad_gate, normed_two, 0, 0).astype(bf)
    raw_up = mm(grad_up, normed_two, 0, 0).astype(bf)
    grad_norm_two = mm(grad_gate, wg, 1, 0) + mm(grad_up, wu, 1, 0)
    grad_middle_part, gain_two_part = jax.vjp(norm_rows, middle, gain_two)[1](grad_norm_two)
    grad_middle = cotangent.astype(jnp.float32) + grad_middle_part
    grad_attn = grad_middle.astype(bf)
    grad_context = mm(grad_attn, wo, 1, 1).astype(bf)
    raw_out = mm(context, grad_attn, 0, 0).astype(bf)

    grad_q, grad_k, grad_v, diag = attend_back(lengths, place, table, q, k, kt, v, context, grad_context, lse, limit, TQ, TK)
    grad_rel = jnp.dot(hot.T, diag.reshape(heads, -1).T, precision=HIGH)
    raw_q = mm(grad_q, normed_one, 0, 0).astype(bf)
    raw_k = mm(grad_k, rows_one, 0, 0).astype(bf)
    raw_v = mm(grad_v, rows_one, 0, 0).astype(bf)
    grad_rows = (mm(grad_k, wk, 1, 0) + mm(grad_v, wv, 1, 0)).astype(bf)
    own_part = mm(grad_q, wq, 1, 0)
    gain_one_part = (
        jnp.sum(grad_rows.astype(jnp.float32) * rows_one.astype(jnp.float32), axis=0)
        + jnp.sum(own_part * normed_one.astype(jnp.float32), axis=0)
    ) / gain_one

    rel_rows = -(-(kinds * heads) // width)
    rel_flat = jnp.pad(grad_rel.reshape(-1), (0, rel_rows * width - kinds * heads)).reshape(rel_rows, width)
    small = jnp.concatenate([gain_one_part[None], gain_two_part[None], rel_flat], axis=0)
    small_rows = -(-small.shape[0] // 8) * 8
    small = jnp.pad(small, ((0, small_rows - small.shape[0]), (0, 0)))
    scale = (total * batches) ** -0.5
    one_group = batches == GROUP
    half = inner // 2
    part = hidden_rows // GROUP
    grads_a = jnp.stack([raw_q, raw_k, raw_v, raw_out]).reshape(2, 2, count, 2, half, width)
    grads_f = [one.reshape(count, 2, 2, 2, part, width) for one in (raw_gate, raw_up, raw_down)]
    grad_norm_one, full_a, full_f, side, summed = reduce(
        grad_rows.reshape(count, own, width), grads_a, grads_f, small, count, radius, scale, one_group
    )
    full_a = full_a.reshape(4, inner, width)
    full_f = full_f.reshape(3, hidden_rows, width)
    summed = summed * scale
    if not one_group:
        full_a, full_f, summed = lax.psum((full_a, full_f, summed), "batch")
        full_a, full_f, summed = full_a * (scale / GROUP), full_f * (scale / GROUP), summed / GROUP
        side = lax.psum(jnp.concatenate([jnp.sum(full_a * full_a, axis=1), jnp.sum(full_f * full_f, axis=1)]), "mp")
    grad_input_part = jax.vjp(lambda one: norm_rows(one, gain_one), inputs)[1](grad_norm_one + own_part)[0]
    grad_tokens = (grad_middle + grad_input_part).astype(bf)

    inner_total = float(inner * count)
    hidden_total = float(hidden_rows * count)
    stat_model = jnp.stack([side[0] / inner_total, side[1] / inner_total, side[2] / inner_total, side[3] / inner_total, side[6] / hidden_total]) + TINY
    stat_ffn_rows = side[4:6] / hidden_total + TINY
    stat_heads = jnp.mean(full_a * full_a, axis=2) + TINY
    stat_hidden = jnp.mean(full_f * full_f, axis=2) + TINY
    rel_sum = summed[2 : 2 + rel_rows].reshape(-1)[: kinds * heads].reshape(kinds, heads)
    rel_own = lax.dynamic_slice_in_dim(rel_sum, lax.axis_index("mp") * rel_table.shape[1], rel_table.shape[1], 1)
    return (
        layer_out,
        grad_tokens,
        full_a[0].T,
        full_a[1].T,
        full_a[2].T,
        full_a[3],
        full_f[0].T,
        full_f[1].T,
        full_f[2],
        rel_own,
        summed[0],
        summed[1],
        stat_model,
        stat_heads,
        stat_hidden,
        stat_ffn_rows,
    )


TQ = 256
TK = 256


def solution(mesh):
    in_specs = (
        P(("batch", "mp"), None),
        P(("batch", "mp"), None),
        P("batch", None),
        P(),
        P(None, "mp"),
        P(None, "mp"),
        P(None, "mp"),
        P("mp", None),
        P(None, "mp"),
        P(None, "mp"),
        P("mp", None),
        P(None, "mp"),
        P(),
        P(),
    )
    out_specs = (
        P(("batch", "mp"), None),
        P(("batch", "mp"), None),
        P(None, "mp"),
        P(None, "mp"),
        P(None, "mp"),
        P("mp", None),
        P(None, "mp"),
        P(None, "mp"),
        P("mp", None),
        P(None, "mp"),
        P(),
        P(),
        P(),
        P(None, "mp"),
        P(None, "mp"),
        P(),
    )
    return jax.shard_map(
        on_device, mesh=mesh, in_specs=in_specs, out_specs=out_specs, check_vma=False
    )
```

time: 1840 us -> 461 us (0.25)
  local copies, waits for them, and re-layouts: 879 us -> 33 us
  waiting for transfers between devices: 460 us -> 0 us
  Pallas kernels: 0 us -> 315 us
  matrix products: 266 us -> 74.1 us
  other arithmetic: 115 us -> 16.6 us
  loops' own time: 40.5 us -> 0 us
  blocking collectives: 44.6 us -> 12.3 us
    while x32 -> x0, local copies, waits for them, and re-layouts: 440 us -> none
    pallas_call x0 -> x4, Pallas kernels: none -> 315 us  [the longest x1 138 us: reduce(): pl.pallas_call(functools.partial(reduce_kernel, count, radius, scale, fin...]
    dot_general x51 -> x25, matrix products: 266 us -> 74.1 us  [the longest x23 71.1 us: mm(): lax.dot_general(a, b, (((ca,), (cb,)), ((), ())), preferred_element_type=...]
    reduce_scatter x4 -> x0, waiting for transfers between devices: 189 us -> none  [the longest x1 63.1 us: on_device(): lax.psum_scatter(jnp.dot(context, w_out, preferred_element_type=jnp.float...]
    reshape x10 -> x6, local copies, waits for them, and re-layouts: 183 us -> 1.04 us  [the longest x1 0.74 us: on_device(): table = jnp.dot(hot, rel_all, precision=HIGH).T.reshape(heads // 2, 2, -1)]
    all_gather x4 -> x0, waiting for transfers between devices: 168 us -> none  [the longest x1 62.8 us: on_device(): rows_two = lax.all_gather(normed_two, 'mp', axis=0, tiled=True)]
    gather x8 -> x0, local copies, waits for them, and re-layouts: 109 us -> none  [bucket_onehot(): kind_ids = buckets[jnp.clip(offsets, 0, 2 * limit - 2)]]
    psum x1 -> x0, waiting for transfers between devices: 102 us -> none  [on_device(): lax.psum((grad_w_query, grad_w_key, grad_w_value, grad_w_out, grad_w_gate...]
  transfers between devices with their start and end apart: 9 -> 0, of which waited for: 8 -> 0; matrix products, arithmetic and copies ran while one was open for 34% -> 0% of each run, Pallas kernels for 0% -> 0%
where the time goes in v1:
time: 461 us; the launch traced here: 453 us
  Pallas kernels  315 us (68%)
  matrix products  74.1 us (16%)
  local copies, waits for them, and re-layouts  33 us (7%)
  other arithmetic  16.6 us (4%)
  blocking collectives  12.3 us (3%)
    pallas_call x1, Pallas kernels, reduce(): pl.pallas_call(functools.partial(reduce_kernel, count, radius, scale, fin...  138 us
    pallas_call x1, Pallas kernels, gather(): pl.pallas_call(functools.partial(gather_kernel, count, radius), in_specs=...  81.2 us
    dot_general x23, matrix products, mm(): lax.dot_general(a, b, (((ca,), (cb,)), ((), ())), preferred_element_type=...  71.1 us
    pallas_call x1, Pallas kernels, attend_back(): pl.pallas_call(functools.partial(bwd_kernel, cfg), grid=(pairs,), in_spec...  52.2 us
    pallas_call x1, Pallas kernels, attend(): pl.pallas_call(functools.partial(fwd_kernel, cfg), grid=(pairs,), in_spec...  43.5 us
    all_gather x1, blocking collectives, on_device(): rel_all = lax.all_gather(rel_table, 'mp', axis=1, tiled=True)  12.3 us

profile of v1, /device:TPU:0, one launch (start us, length us, event | category | flops | bytes accessed | tf_op | source)
XLA Modules:
  0.0 452.5 jit_solution(3399690635140946237)
XLA Ops:
  0.7 1.4 fusion.11
  2.1 1.5 fusion.13.x_ref
  3.6 0.3 copy.43
  3.9 1.4 copy.44
  5.6 0.7 copy-done.28
  6.6 81.2 %gather.1 = (bf16[4,512,768]{2,1,0:T(8,128)(2,1)S(1)}, bf16[4,4,2,96,768]{4,3,2,1,0:T(8,128)(2,1)S(1)}, bf16[3,4,8,64,768]{4,3,2,1,0:T(8,128)(2,1)S(1)}) custom-call(bf16[512,768]{1,0:T(8,128)(2,1)S(1)} %fusion.13.x_ref, bf16[4,2,96,768]{3,2,1,0:T(8,128)(2,1)S(1)} %bitcast.108, bf16[3,8,64,768]{3,2,1,0:T(8,128)(2,1)S(1)} %pad_maximum_fusion.1.wf_ref), custom_call_target="tpu_custom_call" | custom-call | tf_op jit(solution)/shard_map/gather/pallas_call | solution.py:471
  87.8 0.4 fusion.30
  88.3 3.2 copy-done
  91.5 4.0 convolution_convert_fusion.6.k_ref
  95.6 4.1 convolution_convert_fusion.5.vt_ref
  99.6 1.7 convolution_convert_fusion.12.q_ref
  101.3 0.6 fusion.32
  101.9 0.6 broadcast_in_dim.15
  102.6 0.6 broadcast_in_dim.17
  103.5 12.3 %all-gather = f32[4,3,32]{2,1,0:T(4,128)S(1)} all-gather(f32[1,3,32]{2,1,0:T(4,128)S(1)} %bitcast.154), channel_id=1, replica_groups=mesh['batch'=8,'mp'=4] {'mp'}, dimensions={0}, use_global_device_ids=true | all-gather | bytes 1920 | tf_op jit(solution)/shard_map/all_gather | solution.py:823
  115.8 1.7 convolution_bitcast_fusion
  117.5 0.7 reshape.164.table_ref
  118.3 43.5 %attend.1 = (bf16[512,768]{1,0:T(8,128)(2,1)}, f32[6,2,512]{2,1,0:T(2,128)}) custom-call(s32[1,6]{1,0:T(1,128)} %lens_ref.3, s32[1]{0:T(128)} %bitcast.place_ref, f32[6,2,2560]{2,1,0:T(2,128)} %reshape.164.table_ref, bf16[512,768]{1,0:T(8,128)(2,1)} %convolution_convert_fusion.12.q_ref, bf16[2048,768]{1,0:T(8,128)(2,1)} %convolution_convert_fusion.6.k_ref, ...), custom_call_target="tpu_custom_call" | custom-call | tf_op jit(solution)/shard_map/attend/pallas_call | solution.py:138
  161.8 2.0 multiply_reduce_fusion.6
  164.0 4.7 %fusion.28 = (bf16[1,4,8,64,768]{4,3,2,1,0:T(8,128)(2,1)S(1)}, bf16[1,4,8,64,768]{4,3,2,1,0:T(8,128)(2,1)S(1)}, bf16[1,4,8,64,768]{4,3,2,1,0:T(8,128)(2,1)S(1)}) fusion(bf16[3,4,8,64,768]{4,3,2,1,0:T(8,128)(2,1)} %copy-done), kind=kLoop, calls=%fused_computation.92 | loop fusion | bytes 18874368 | tf_op jit(solution)/shard_map/slice | solution.py:832
  168.8 1.8 fusion.34
  170.6 1.8 fusion.33
  172.5 6.5 %fusion.7 = (bf16[512,2048]{1,0:T(8,128)(2,1)S(1)}, bf16[512,2048]{1,0:T(8,128)(2,1)S(1)}, bf16[512,2048]{1,0:T(8,128)(2,1)}) fusion(f32[512,2048]{1,0:T(8,128)S(1)} %fusion.33, f32[512,2048]{1,0:T(8,128)S(1)} %fusion.34, bf16[2048,768]{1,0:T(8,128)(2,1)S(1)} %bitcast.120, bf16[512,768]{1,0:T(8,128)(2,1)S(1)} %copy-done.26), kind=kOutput, calls=%fused_computation.15 | convolution fusion | flops 1637875712 | bytes 18612224 | tf_op jit(solution)/shard_map/dot_general | solution.py:802
  179.0 1.8 fusion.35
  181.0 2.1 multiply_reduce_fusion.3
  183.1 0.4 fusion.8
  183.5 0.8 copy-done.20
  184.4 1.7 convolution_convert_fusion.11.do_ref
  186.1 0.4 copy-done.2
  186.5 4.2 convolution_convert_fusion.3.v_ref
  190.7 4.0 convolution_convert_fusion.4.kt_ref
  194.8 52.2 %attend_back.1 = (bf16[512,768]{1,0:T(8,128)(2,1)}, bf16[2048,768]{1,0:T(8,128)(2,1)}, bf16[2048,768]{1,0:T(8,128)(2,1)}, f32[6,2,2560]{2,1,0:T(2,128)}) custom-call(s32[1,6]{1,0:T(1,128)} %lens_ref.3, s32[1]{0:T(128)} %bitcast.place_ref, f32[6,2,2560]{2,1,0:T(2,128)} %reshape.164.table_ref, bf16[512,768]{1,0:T(8,128)(2,1)} %convolution_convert_fusion.12.q_ref, ...), custom_call_target="tpu_custom_call" | custom-call | tf_op jit(solution)/shard_map/attend_back/pallas_call | solution.py:232
  247.0 3.2 multiply_reduce_fusion.4
  250.2 2.6 fusion.36
  252.9 4.6 %multiply_reduce_fusion = (f32[768]{0:T(1024)S(1)}, bf16[2048,768]{1,0:T(8,128)(2,1)}) fusion(bf16[4,512,768]{2,1,0:T(8,128)(2,1)S(1)} %copy-done.2, f32[2048,768]{1,0:T(8,128)S(1)} %fusion.36, bf16[2048,768]{1,0:T(8,128)(2,1)S(1)} %copy-done.38, bf16[768,768]{1,0:T(8,128)(2,1)S(1)} %bitcast.137), kind=kOutput, calls=%fused_computation | convolution fusion | flops 2425355520 | bytes 16911360 | tf_op jit(solution)/shard_map/dot_general | solution.py:802
  257.7 1.2 fusion.20
  259.1 0.6 select_maximum_fusion.small_ref
  259.7 5.5 %convolution_convert_fusion.2 = bf16[2048,768]{1,0:T(8,128)(2,1)} fusion(bf16[512,2048]{1,0:T(8,128)(2,1)} %copy-done.45, bf16[512,768]{1,0:T(8,128)(2,1)} %copy-done.24), kind=kOutput, calls=%fused_computation.20 | convolution fusion | flops 1612185600 | bytes 6029312 | tf_op jit(solution)/shard_map/dot_general | solution.py:802
  265.2 3.6 convolution_convert_fusion.1
  268.8 2.7 fusion.17
  271.5 2.7 fusion.18
  274.3 0.8 fusion.16
  275.1 0.3 copy-done.22
  275.4 0.8 fusion.15
  276.3 2.7 pad_maximum_fusion
  279.0 0.3 copy-done.44
  279.4 3.5 convolution_convert_fusion
  282.9 137.8 %reduce.9 = (f32[512,768]{1,0:T(8,128)}, f32[4,2,96,768]{3,2,1,0:T(8,128)}, f32[3,8,64,768]{3,2,1,0:T(8,128)}, f32[8,768]{1,0:T(8,128)}, f32[8,768]{1,0:T(8,128)}) custom-call(bf16[4,512,768]{2,1,0:T(8,128)(2,1)} %bitcast.122, bf16[2,2,4,2,96,768]{5,4,3,2,1,0:T(8,128)(2,1)} %bitcast.115, bf16[4,2,2,2,64,768]{5,4,3,2,1,0:T(8,128)(2,1)} %bitcast.123, ...), custom_call_target="tpu_custom_call" | custom-call | tf_op jit(solution)/shard_map/reduce/pallas_call | solution.py:769
  420.7 1.0 slice_multiply_fusion
  421.7 0.6 broadcast_add_fusion
  422.4 4.6 %fusion.29 = (f32[1,8,64,768]{3,2,1,0:T(8,128)}, f32[1,8,64,768]{3,2,1,0:T(8,128)}, f32[1,8,64,768]{3,2,1,0:T(8,128)}) fusion(f32[3,8,64,768]{3,2,1,0:T(8,128)} %get-tuple-element.41), kind=kLoop, calls=%fused_computation.93 | loop fusion | bytes 9437184 | tf_op jit(solution)/shard_map/slice | solution.py:918
  427.0 3.0 copy.47
  430.0 3.0 copy.48
  433.0 3.2 fusion.31
  436.2 0.4 fusion.14
  436.6 1.4 fusion.10
  438.3 0.7 copy.49
  438.9 0.6 slice_reduce_fusion
  439.5 2.7 multiply_reduce_fusion.1
  442.3 0.7 add.110
  442.9 1.9 multiply_reduce_fusion.2
  444.9 0.7 add.107
  445.5 1.3 multiply_add_fusion.1
  446.9 5.2 %add_convert_fusion.1 = bf16[512,768]{1,0:T(8,128)(2,1)} fusion(f32[512,768]{1,0:T(8,128)S(1)} %copy-done.8, bf16[512,2048]{1,0:T(8,128)(2,1)} %get-tuple-element.85, bf16[2048,768]{1,0:T(8,128)(2,1)} %bitcast.121), kind=kOutput, calls=%fused_computation.46 | convolution fusion | flops 1611399168 | bytes 7602176 | tf_op jit(solution)/shard_map/dot_general | solution.py:802
  (111 shorter events, 1.9 us)
Async XLA Ops:
  0.6 2.9 copy-start.23
  2.1 3.2 copy-start.21
  5.3 1.0 copy-start.28
  5.3 1.0 copy-start.29
  5.3 1.1 copy-start.30
  5.3 1.2 copy-start.31
  87.8 3.7 copy-start
  87.8 7.7 %copy-start.1 = (bf16[4,512,768]{2,1,0:T(8,128)(2,1)}, bf16[4,512,768]{2,1,0:T(8,128)(2,1)S(1)}, u32[]{:S(2)}) copy-start(bf16[4,512,768]{2,1,0:T(8,128)(2,1)S(1)} %get-tuple-element.31) | copy-start | bytes 9437188
  91.5 4.1 copy-start.16
  91.5 4.1 copy-start.13
  91.5 8.1 %copy-start.9 = (bf16[1,4,2,96,768]{4,3,2,1,0:T(8,128)(2,1)}, bf16[1,4,2,96,768]{4,3,2,1,0:T(8,128)(2,1)S(1)}, u32[]{:S(2)}) copy-start(bf16[1,4,2,96,768]{4,3,2,1,0:T(8,128)(2,1)S(1)} %get-tuple-element.92) | copy-start | bytes 3538948
  91.5 70.3 %copy-start.19 = (bf16[1,4,2,96,768]{4,3,2,1,0:T(8,128)(2,1)}, bf16[1,4,2,96,768]{4,3,2,1,0:T(8,128)(2,1)S(1)}, u32[]{:S(2)}) copy-start(bf16[1,4,2,96,768]{4,3,2,1,0:T(8,128)(2,1)S(1)} %get-tuple-element.89) | copy-start | bytes 3538948
  99.6 1.7 copy-start.36
  99.6 3.8 copy-start.37
  118.3 43.5 %copy-start.5 = (bf16[512,768]{1,0:T(8,128)(2,1)S(1)}, bf16[512,768]{1,0:T(8,128)(2,1)}, u32[]{:S(2)}) copy-start(bf16[512,768]{1,0:T(8,128)(2,1)} %param.14) | copy-start | bytes 2359300
  161.8 2.0 copy-start.35
  163.8 19.3 %copy-start.7 = (f32[512,768]{1,0:T(8,128)}, f32[512,768]{1,0:T(8,128)S(1)}, u32[]{:S(2)}) copy-start(f32[512,768]{1,0:T(8,128)S(1)} %get-tuple-element.105) | copy-start | bytes 4718596
  164.0 6.6 %copy-start.24 = (bf16[512,768]{1,0:T(8,128)(2,1)}, bf16[512,768]{1,0:T(8,128)(2,1)S(1)}, u32[]{:S(2)}) copy-start(bf16[512,768]{1,0:T(8,128)(2,1)S(1)} %multiply_convert_fusion.1) | copy-start | bytes 2359300
  168.8 3.7 copy-start.11
  170.6 1.9 copy-start.26
  179.0 1.8 copy-start.45
  179.0 2.0 copy-start.42
  183.1 1.3 copy-start.20
  183.1 3.0 copy-start.14
  184.3 2.2 copy-start.2
  186.5 4.2 copy-start.17
  194.8 52.2 %copy-start.10 = (bf16[1,4,2,96,768]{4,3,2,1,0:T(8,128)(2,1)S(1)}, bf16[1,4,2,96,768]{4,3,2,1,0:T(8,128)(2,1)}, u32[]{:S(2)}) copy-start(bf16[1,4,2,96,768]{4,3,2,1,0:T(8,128)(2,1)} %copy-done.9) | copy-start | bytes 3538948
  247.0 3.2 copy-start.18
  247.0 3.2 copy-start.40
  250.2 2.6 copy-start.15
  250.2 2.6 copy-start.38
  252.9 4.7 %copy-start.33 = (f32[768]{0:T(1024)S(1)}, f32[768]{0:T(1024)}, u32[]{:S(2)}) copy-start(f32[768]{0:T(1024)} %param.26) | copy-start | bytes 9220
  252.9 4.7 %copy-start.32 = (f32[6,2,2560]{2,1,0:T(2,128)S(1)}, f32[6,2,2560]{2,1,0:T(2,128)}, u32[]{:S(2)}) copy-start(f32[6,2,2560]{2,1,0:T(2,128)} %get-tuple-element.38) | copy-start | bytes 368644
  259.7 5.5 %copy-start.25 = (bf16[512,768]{1,0:T(8,128)(2,1)S(1)}, bf16[512,768]{1,0:T(8,128)(2,1)}, u32[]{:S(2)}) copy-start(bf16[512,768]{1,0:T(8,128)(2,1)} %copy-done.24) | copy-start | bytes 2359300
  259.7 5.5 %copy-start.43 = (bf16[512,2048]{1,0:T(8,128)(2,1)S(1)}, bf16[512,2048]{1,0:T(8,128)(2,1)}, u32[]{:S(2)}) copy-start(bf16[512,2048]{1,0:T(8,128)(2,1)} %copy-done.42) | copy-start | bytes 6291460
  265.2 3.6 copy-start.3
  265.2 3.6 copy-start.41
  268.8 2.7 copy-start.39
  271.5 2.8 copy-start.12
  274.3 1.1 copy-start.22
  276.2 2.8 copy-start.27
  276.2 3.1 copy-start.44
  433.0 3.2 copy-start.4
  433.0 3.2 copy-start.6
  436.6 1.4 copy-start.34
  442.2 4.6 %copy-start.8 = (f32[512,768]{1,0:T(8,128)S(1)}, f32[512,768]{1,0:T(8,128)}, u32[]{:S(2)}) copy-start(f32[512,768]{1,0:T(8,128)} %copy-done.7) | copy-start | bytes 4718596
